TPU v7x, 512 devices: a whole 4x8x8 slice. The times are simulated.
512 devices in a mesh: sp: 128 (over y, z, core), tp: 4 (over x).
Axes of the slice: x: 4, y: 8, z: 8, core: 2. Of those that a mesh axis runs over, the one named last changes fastest.
Arguments:
- prefilled_block_keys: bfloat16 [8192, 8, 1024], P(('sp', 'tp')), may hold values from -4 to 4
- prefilled_block_values: bfloat16 [8192, 8, 1024], P(('sp', 'tp')), may hold values from -6 to 6
- queries: bfloat16 [4, 4, 8192], P(None, None, 'tp'), may hold values from -128 to 128
- step_token_keys: bfloat16 [4, 4, 1024], P(None, None, 'tp'), may hold values from -32 to 32
- step_token_values: bfloat16 [4, 4, 1024], P(None, None, 'tp'), may hold values from -6 to 6
- lengths: int32 [4], replicated, may hold values from 8185 to 40960, as said below
- block_request: int32 [8192], P(('sp', 'tp')), may hold values from 0 to 3, as said below
- block_number: int32 [8192], P(('sp', 'tp')), may hold values from 0 to 5119
- owner_rank: int32 [8192], P(('sp', 'tp')), may hold values from 0 to 79, as said below
- owner_slot: int32 [8192], P(('sp', 'tp')), may hold values from 0 to 127, as said below
- group_first: int32 [4], replicated, may hold values from 0 to 112, as said below
Outputs:
- attended: float32 [4, 4, 8192], P(None, None, 'tp')
- log_norm: float32 [4, 4, 64], P(None, None, 'tp')
- owner_slot_keys: bfloat16 [16384, 8, 1024], P('sp', None, 'tp')
- owner_slot_values: bfloat16 [16384, 8, 1024], P('sp', None, 'tp')
Inputs may be any that keep to these rules, and one draw needn't show every extreme that they name: `lengths`: each request's length lies in its last block: with n blocks, 8 * (n - 1) < length <= 8 * n. `block_request`: every request has blocks, and its blocks carry the numbers 0 to n - 1 once each. The owner group_first + owner_rank lies in the request's group. `owner_slot`: no two blocks share an owner and a slot; the 64 blocks of one index of sp in the prefill layout reach one owner at most 1 times, and this is reached. `group_first`: the groups are runs of indices of sp, one for each request in some order, that do not meet and cover the whole axis.
All inputs are finite; a program needn't handle non-finite values.
Results may differ from a plain program's by a relative error of at most 0.0004.
Values may be sent and summed in bfloat16 or wider, within the bound.
A program may use at most 64 MiB of HBM per device.

v0:
```python
import math

import jax
import jax.numpy as jnp
from jax import lax
from jax.sharding import PartitionSpec as P

HEAD_SIZE = 128


NEGATIVE = -1e30


def lookup(small_table, indices):
    hits = indices[..., None] == jnp.arange(small_table.shape[0], dtype=jnp.int32)
    return jnp.sum(jnp.where(hits, small_table, 0), axis=-1)


def earlier_same(owners):
    width_count = owners.shape[-1]
    alike = owners[..., :, None] == owners[..., None, :]
    before = jnp.arange(width_count)[None, :] < jnp.arange(width_count)[:, None]
    return jnp.sum(alike & before, axis=-1)


def attend(
    key_blocks,
    value_blocks,
    token_request,
    token_position,
    queries,
    step_token_keys,
    step_token_values,
    lengths,
):
    steps, requests, query_width = queries.shape
    kv_local = key_blocks.shape[-1] // HEAD_SIZE
    queries_per_group = query_width // HEAD_SIZE // kv_local
    tokens = key_blocks.shape[0] * key_blocks.shape[1]
    score_scale = 1.0 / math.sqrt(HEAD_SIZE)
    key_matrix = key_blocks.reshape(tokens, kv_local, HEAD_SIZE)
    value_matrix = value_blocks.reshape(tokens, kv_local, HEAD_SIZE)
    query_matrix = queries.reshape(steps, requests, kv_local, queries_per_group, HEAD_SIZE)
    current_keys = step_token_keys.reshape(steps, requests, kv_local, HEAD_SIZE)
    current_values = step_token_values.reshape(steps, requests, kv_local, HEAD_SIZE)
    within_length = token_position < lookup(lengths, token_request)
    allowed_mask = (
        token_request[None, :] == jnp.arange(requests, dtype=jnp.int32)[:, None]
    ) & within_length[None, :]
    cache_allowed = allowed_mask[None, :, None, None, :]
    causal = (jnp.arange(steps)[None, :] <= jnp.arange(steps)[:, None])[:, None, None, None, :]
    scores = (
        jnp.einsum("srhgd,thd->srhgt", query_matrix, key_matrix, preferred_element_type=jnp.float32)
        * score_scale
    )
    fresh_scores = (
        jnp.einsum(
            "srhgd,jrhd->srhgj", query_matrix, current_keys, preferred_element_type=jnp.float32
        )
        * score_scale
    )
    local_top = jnp.maximum(
        jnp.max(jnp.where(cache_allowed, scores, NEGATIVE), axis=-1),
        jnp.max(jnp.where(causal, fresh_scores, NEGATIVE), axis=-1),
    )
    row_top = lax.pmax(local_top, "sp")
    weights = jnp.where(cache_allowed, jnp.exp(scores - row_top[..., None]), 0.0)
    weight_sum = jnp.sum(weights, axis=-1)
    numerator = jnp.einsum(
        "srhgt,thd->srhgd",
        weights.astype(jnp.bfloat16),
        value_matrix,
        preferred_element_type=jnp.float32,
    )
    numerator, weight_sum = lax.psum((numerator, weight_sum), "sp")
    fresh_weights = jnp.where(causal, jnp.exp(fresh_scores - row_top[..., None]), 0.0)
    totals = weight_sum + jnp.sum(fresh_weights, axis=-1)
    numerator = numerator + jnp.einsum(
        "srhgj,jrhd->srhgd",
        fresh_weights.astype(jnp.bfloat16),
        current_values,
        preferred_element_type=jnp.float32,
    )
    attended = (numerator / totals[..., None]).reshape(steps, requests, query_width)
    log_norm = (row_top + jnp.log(totals)).reshape(steps, requests, kv_local * queries_per_group)
    return (attended, log_norm)


def on_device(
    prefilled_block_keys,
    prefilled_block_values,
    queries,
    step_token_keys,
    step_token_values,
    lengths,
    block_request,
    block_number,
    owner_rank,
    owner_slot,
    group_first,
):
    sp_count = lax.axis_size("sp")
    tp_count = lax.axis_size("tp")
    own_blocks, block_len, full_width = prefilled_block_keys.shape
    piece_width = full_width // tp_count
    row_blocks = own_blocks * tp_count
    slot_count = 2 * row_blocks
    pair_cap = max(1, slot_count // sp_count)
    my_row = lax.axis_index("sp")
    block_tables = jnp.stack([block_request, block_number, owner_rank, owner_slot], axis=1)
    gathered = lax.all_gather(block_tables, ("sp", "tp"), axis=0, tiled=True).reshape(
        sp_count, row_blocks, 4
    )
    all_owner = lookup(group_first, gathered[..., 0]) + gathered[..., 2]
    split_keys = prefilled_block_keys.reshape(own_blocks, block_len, tp_count, piece_width)
    split_values = prefilled_block_values.reshape(own_blocks, block_len, tp_count, piece_width)
    row_keys, row_values = (
        lax.all_to_all(split_keys, "tp", split_axis=2, concat_axis=0, tiled=True),
        lax.all_to_all(split_values, "tp", split_axis=2, concat_axis=0, tiled=True),
    )
    row_keys = row_keys.reshape(row_blocks, block_len, piece_width)
    row_values = row_values.reshape(row_blocks, block_len, piece_width)
    row_owner = lax.dynamic_index_in_dim(all_owner, my_row, 0, keepdims=False)
    send_index = row_owner * pair_cap + earlier_same(row_owner)
    wanted = send_index[None, :] == jnp.arange(sp_count * pair_cap, dtype=jnp.int32)[:, None]
    source = jnp.sum(jnp.where(wanted, jnp.arange(row_blocks, dtype=jnp.int32)[None, :], 0), axis=1)
    present = jnp.any(wanted, axis=1)[:, None, None]
    empty_value = jnp.zeros((), jnp.bfloat16)
    send_keys = jnp.where(present, jnp.take(row_keys, source, axis=0), empty_value)
    send_values = jnp.where(present, jnp.take(row_values, source, axis=0), empty_value)
    got_keys, got_values = (
        lax.all_to_all(send_keys, "sp", split_axis=0, concat_axis=0, tiled=True),
        lax.all_to_all(send_values, "sp", split_axis=0, concat_axis=0, tiled=True),
    )
    incoming = jnp.arange(sp_count, dtype=jnp.int32)[:, None] * pair_cap + earlier_same(all_owner)
    owned_here = (all_owner == my_row).reshape(-1)
    matches = owned_here[None, :] & (
        gathered[..., 3].reshape(-1)[None, :] == jnp.arange(slot_count, dtype=jnp.int32)[:, None]
    )
    arrival = jnp.sum(jnp.where(matches, incoming.reshape(-1)[None, :], 0), axis=1)
    filled = jnp.any(matches, axis=1)
    slot_request = jnp.where(
        filled, jnp.sum(jnp.where(matches, gathered[..., 0].reshape(-1)[None, :], 0), axis=1), -1
    )
    slot_number = jnp.sum(jnp.where(matches, gathered[..., 1].reshape(-1)[None, :], 0), axis=1)
    owner_slot_keys = jnp.where(
        filled[:, None, None], jnp.take(got_keys, arrival, axis=0), empty_value
    )
    owner_slot_values = jnp.where(
        filled[:, None, None], jnp.take(got_values, arrival, axis=0), empty_value
    )
    offsets = jnp.arange(block_len, dtype=jnp.int32)[None, :]
    token_request = jnp.repeat(slot_request, block_len, total_repeat_length=slot_count * block_len)
    token_position = (slot_number[:, None] * block_len + offsets).reshape(-1)
    attended, log_norm = attend(
        owner_slot_keys,
        owner_slot_values,
        token_request,
        token_position,
        queries,
        step_token_keys,
        step_token_values,
        lengths,
    )
    return (attended, log_norm, owner_slot_keys, owner_slot_values)


def solution(mesh):
    return jax.shard_map(
        on_device,
        mesh=mesh,
        in_specs=(
            P(("sp", "tp"), None, None),
            P(("sp", "tp"), None, None),
            P(None, None, "tp"),
            P(None, None, "tp"),
            P(None, None, "tp"),
            P(),
            P(("sp", "tp")),
            P(("sp", "tp")),
            P(("sp", "tp")),
            P(("sp", "tp")),
            P(),
        ),
        out_specs=(
            P(None, None, "tp"),
            P(None, None, "tp"),
            P("sp", None, "tp"),
            P("sp", None, "tp"),
        ),
        check_vma=False,
    )
```

profile of v0, /device:TPU:1, one launch (start us, length us, event | category | flops | bytes accessed | tf_op | source)
XLA Modules:
  0.0 1391.8 jit_solution(11877630832900269052)
XLA Ops:
  7.2 1.7 copy.174
  8.9 4.8 all-to-all-start.2
  13.8 132.5 %all-gather = s32[512,16,4]{1,2,0:T(4,128)S(1)} all-gather(s32[1,16,4]{1,2,0:T(4,128)S(1)} %add_bitcast_fusion), channel_id=1, replica_groups=mesh['sp'=128,'tp'=4] {'sp','tp'}, dimensions={0}, use_global_device_ids=true | all-gather | bytes 131328 | tf_op jit(solution)/shard_map/all_gather | solution.py:111
  146.4 0.3 reshape.280
  148.2 0.7 copy.175
  148.9 0.7 convert_reduce_fusion
  150.2 2.5 select_reduce_fusion
  152.7 3.4 all-to-all-start
  156.2 0.6 fusion.1
  156.8 0.7 gather_fusion.3
  157.5 4.2 all-to-all-done
  161.6 0.6 gather_fusion.1
  162.3 1.5 select_select_fusion.3
  163.8 11.1 all-to-all-start.3
  175.0 6.6 gather_fusion
  181.9 12.5 all-to-all-done.3
  194.4 7.2 all-to-all-start.1
  202.2 0.4 select_reduce_fusion.5
  202.6 0.6 gather_fusion.4
  203.3 18.0 %all-to-all-done.1 = bf16[128,8,256]{2,1,0:T(8,128)(2,1)S(1)} async-done(((bf16[128,8,256]{2,1,0:T(8,128)(2,1)}), bf16[128,8,256]{2,1,0:T(8,128)(2,1)S(1)}, u32[]{:S(2)}, u32[]{:S(2)}) %all-to-all-start.1) | async-done | bytes 524320 | tf_op jit(solution)/shard_map/all_to_all | solution.py:133
  221.3 0.6 gather_fusion.2
  221.9 0.7 select_select_fusion.2
  222.8 0.4 select_reduce_fusion.3
  223.2 0.2 copy-done.1
  223.5 487.2 %pmax.7 = f32[4,4,2,8]{3,1,0,2:T(4,128)S(1)} all-reduce(f32[4,4,2,8]{3,1,0,2:T(4,128)S(1)} %copy_maximum_fusion), channel_id=1, replica_groups=mesh['sp'=128,'tp'=4] {'sp'}, use_global_device_ids=true, to_apply=%region_12.15 | all-reduce | flops 256 | bytes 2048 | tf_op jit(solution)/shard_map/pmax | solution.py:66
  710.6 0.3 fusion.6
  711.0 490.9 %psum.15 = f32[4,4,2,8]{3,1,0,2:T(4,128)S(1)} all-reduce(f32[4,4,2,8]{3,1,0,2:T(4,128)S(1)} %fusion.6), channel_id=1, replica_groups=mesh['sp'=128,'tp'=4] {'sp'}, use_global_device_ids=true, to_apply=%region_15.18 | all-reduce | flops 256 | bytes 2048 | tf_op jit(solution)/shard_map/psum | solution.py:75
  1202.0 1.0 convolution_bitcast_fusion
  1203.2 0.7 reshape.291
  1203.9 179.2 %all-reduce.2.cloned.1.call-done = f32[4,4,2,8,128]{4,3,1,0,2:T(8,128)} async-done(((f32[4,4,2,8,128]{4,3,1,0,2:T(8,128)}), f32[4,4,2,8,128]{4,3,1,0,2:T(8,128)}) %all-reduce.2.cloned.1.call-update) | async-done | bytes 131088 | tf_op jit(solution)/shard_map/psum | solution.py:75
  1383.1 1.1 fusion.4
  1384.3 0.7 reshape.290
  (82 shorter events, 3.3 us)
Async XLA Ops:
  7.2 6.6 copy-start.12
  7.2 6.6 copy-start.11
  7.2 6.6 copy-start.10
  7.2 6.6 copy-start.9
  8.9 143.8 %all-to-all-start.2 = ((bf16[16,8,4,256]{3,1,0,2:T(8,128)(2,1)}), bf16[16,8,4,256]{3,1,0,2:T(8,128)(2,1)S(1)}, u32[]{:S(2)}, u32[]{:S(2)}) async-start(bf16[16,8,4,256]{3,1,0,2:T(8,128)(2,1)} %bitcast.72), calls=%async_computation.2 | async-start | bytes 524288 | tf_op jit(solution)/shard_map/all_to_all | solution.py:118
  146.3 0.7 copy-start.7
  146.3 1.8 copy-start.2
  146.7 3.4 copy-start.4
  152.7 8.9 all-to-all-start
  163.8 30.6 %all-to-all-start.3 = ((bf16[128,8,256]{2,1,0:T(8,128)(2,1)}), bf16[128,8,256]{2,1,0:T(8,128)(2,1)S(1)}, u32[]{:S(2)}, u32[]{:S(2)}) async-start(bf16[128,8,256]{2,1,0:T(8,128)(2,1)} %get-tuple-element.35), calls=%async_computation.3 | async-start | bytes 1048576 | tf_op jit(solution)/shard_map/all_to_all | solution.py:132
  175.0 6.7 copy-start.8
  181.6 20.4 %copy-start.3 = (bf16[4,4,2048]{2,1,0:T(4,128)(2,1)S(1)}, bf16[4,4,2048]{2,1,0:T(4,128)(2,1)}, u32[]{:S(2)}) copy-start(bf16[4,4,2048]{2,1,0:T(4,128)(2,1)} %param.19) | copy-start | bytes 196612
  181.6 20.5 %copy-start.5 = (bf16[4,4,256]{2,1,0:T(4,128)(2,1)S(1)}, bf16[4,4,256]{2,1,0:T(4,128)(2,1)}, u32[]{:S(2)}) copy-start(bf16[4,4,256]{2,1,0:T(4,128)(2,1)} %param.20) | copy-start | bytes 24580
  181.6 20.5 %copy-start.6 = (bf16[4,4,256]{2,1,0:T(4,128)(2,1)S(1)}, bf16[4,4,256]{2,1,0:T(4,128)(2,1)}, u32[]{:S(2)}) copy-start(bf16[4,4,256]{2,1,0:T(4,128)(2,1)} %param.21) | copy-start | bytes 24580
  194.4 26.8 %all-to-all-start.1 = ((bf16[128,8,256]{2,1,0:T(8,128)(2,1)}), bf16[128,8,256]{2,1,0:T(8,128)(2,1)S(1)}, u32[]{:S(2)}, u32[]{:S(2)}) async-start(bf16[128,8,256]{2,1,0:T(8,128)(2,1)} %get-tuple-element.34), calls=%async_computation.1 | async-start | bytes 1048576 | tf_op jit(solution)/shard_map/all_to_all | solution.py:133
  201.7 1181.4 %all-reduce.2.cloned.1.call-start = ((), (), s32[]{:S(2)}) async-start(), calls=%async_computation.4 | async-start | bytes 262144 | tf_op jit(solution)/shard_map/psum | solution.py:75
  222.7 0.8 copy-start.1
  222.7 979.2 %copy-start = (bf16[128,8,256]{2,1,0:T(8,128)(2,1)}, bf16[128,8,256]{2,1,0:T(8,128)(2,1)S(1)}, u32[]{:S(2)}) copy-start(bf16[128,8,256]{2,1,0:T(8,128)(2,1)S(1)} %get-tuple-element.32) | copy-start | bytes 1572868
Sparse Core Ops, SparseCore 0:
  1203.1 179.9 all-reduce.1
where the time goes:
time: 1390 us
  blocking collectives  1110 us (80%)
  waiting for transfers between devices  214 us (15%)
  starting transfers between devices  26.9 us (2%)
  local copies, waits for them, and re-layouts  15.3 us (1%)
  between operations  14.5 us (1%)
    psum x1, blocking collectives, attend(): numerator, weight_sum = lax.psum((numerator, weight_sum), 'sp')  491 us
    pmax x1, blocking collectives, attend(): row_top = lax.pmax(local_top, 'sp')  487 us
    psum x1, waiting for transfers between devices, attend(): numerator, weight_sum = lax.psum((numerator, weight_sum), 'sp')  179 us
    all_gather x1, blocking collectives, on_device(): lax.all_gather(block_tables, ('sp', 'tp'), axis=0, tiled=True)  132 us
  transfers between devices with their start and end apart: 5, of which 4 were waited for; matrix products, arithmetic and copies ran while one was open for 1% of the time, Pallas kernels for 0%

commit v1 on v0

v1 whole, which is shorter than its diff:
```python
import functools
import math

import jax
import jax.numpy as jnp
from jax import lax
from jax.experimental import pallas as pl
from jax.experimental.pallas import tpu as pltpu
from jax.sharding import PartitionSpec as P

D = 128
TOK = 8
STEPS = 4
REQUESTS = 4
SR = STEPS * REQUESTS
GROUP = 8
ROWS = GROUP * SR
LOCAL_HEADS = 2
PIECE = LOCAL_HEADS * D
NEGATIVE = -1e30
SCALE = 1.0 / math.sqrt(D)
MESH = pl.DeviceIdType.MESH
F32 = jnp.float32
BF16 = jnp.bfloat16
NT = (((1,), (1,)), ((), ()))
TN = (((0,), (0,)), ((), ()))


def exchange_kernel(
    n_y,
    n_zc,
    n_tp,
    own_blocks,
    request_ref,
    number_ref,
    rank_ref,
    slot_ref,
    lengths_ref,
    first_ref,
    q_ref,
    fresh_k_ref,
    fresh_v_ref,
    keys_ref,
    values_ref,
    attended_ref,
    norm_ref,
    arrival_ref,
    kc,
    vc,
    meta,
    kp,
    vp,
    k32,
    v32,
    src_v,
    src_s,
    scores,
    ka,
    kb,
    va,
    vb,
    mx,
    my_msg,
    my_buf,
    fresh_num,
    rs_src,
    rs_buf,
    yy_buf,
    ag_buf,
    local_sem,
    meta_send,
    meta_recv,
    kp_send,
    kp_recv,
    vp_send,
    vp_recv,
    mx_send,
    mx_recv,
    my_send,
    my_recv,
    k1_send,
    k1_recv,
    k2_send,
    k2_recv,
    v1_send,
    v1_recv,
    v2_send,
    v2_recv,
    rs_send,
    rs_recv,
    yy_send,
    yy_recv,
    ag_send,
    ag_recv,
):
    me = lax.axis_index("sp")
    tp = lax.axis_index("tp")
    my = me // n_zc
    mzc = lax.rem(me, n_zc)
    tokens = own_blocks * TOK

    def zc_at(k):
        return lax.rem(mzc + k, n_zc)

    def y_at(j):
        return lax.rem(my + j, n_y)

    def tp_at(k):
        return lax.rem(tp + k, n_tp)

    def zc_dev(k):
        return (my * n_zc + zc_at(k), tp)

    def y_dev(j):
        return (y_at(j) * n_zc + mzc, tp)

    def tp_dev(k):
        return (me, tp_at(k))

    def remote(src, dst, send, recv, dev):
        copy = pltpu.make_async_remote_copy(
            src_ref=src, dst_ref=dst, send_sem=send, recv_sem=recv, device_id=dev, device_id_type=MESH
        )
        copy.start()
        return copy

    barrier = pltpu.get_barrier_semaphore()
    for k in range(1, n_tp):
        pl.semaphore_signal(barrier, inc=1, device_id=tp_dev(k), device_id_type=MESH)
    for k in range(1, n_zc):
        pl.semaphore_signal(barrier, inc=1, device_id=zc_dev(k), device_id_type=MESH)
    for j in range(1, n_y):
        pl.semaphore_signal(barrier, inc=1, device_id=y_dev(j), device_id_type=MESH)

    def columns(t):
        return pl.ds(pl.multiple_of(t * PIECE, PIECE), PIECE)

    own_k = pltpu.make_async_copy(keys_ref.at[:, columns(tp)], kp.at[tp], local_sem.at[0])
    own_v = pltpu.make_async_copy(values_ref.at[:, columns(tp)], vp.at[tp], local_sem.at[1])
    own_k.start()
    own_v.start()

    lane = lax.broadcasted_iota(jnp.int32, (1, D), 1)
    codes = jnp.full((1, D), REQUESTS, jnp.int32)
    sources = jnp.zeros((1, D), jnp.int32)
    slots = jnp.zeros((1, D), jnp.int32)
    for b in range(own_blocks):
        request = request_ref[b]
        owner = first_ref[request] + rank_ref[b]
        place = number_ref[b] * TOK + (lane - b * TOK)
        mine = (lane >= b * TOK) & (lane < (b + 1) * TOK) & (place < lengths_ref[request])
        codes = jnp.where(mine, request, codes)
        hit = lane == owner
        sources = jnp.where(hit, tp * own_blocks + b + 1, sources)
        slots = jnp.where(hit, slot_ref[b] + 1, slots)
    own_meta = jnp.concatenate(
        [codes, sources, slots, jnp.zeros((5, D), jnp.int32)], axis=0
    )
    meta[tp] = own_meta

    row_lane = lax.broadcasted_iota(jnp.int32, (1, ROWS), 1)
    row_request = lax.rem(row_lane, REQUESTS)
    row_step = lax.rem(row_lane, SR) // REQUESTS
    row_code = row_request.astype(F32)

    def q_head(h):
        return jnp.concatenate(
            [q_ref[:, pl.ds((h * GROUP + g) * D, D)] for g in range(GROUP)], axis=0
        )

    fresh_row = lax.broadcasted_iota(jnp.int32, (SR, ROWS), 0)
    fresh_ok = (lax.rem(fresh_row, REQUESTS) == row_request) & (fresh_row // REQUESTS <= row_step)
    fresh_scores = []
    for h in range(LOCAL_HEADS):
        dots = lax.dot_general(
            fresh_k_ref[:, pl.ds(h * D, D)], q_head(h), NT, preferred_element_type=F32
        )
        fresh_scores.append(jnp.where(fresh_ok, dots * SCALE, NEGATIVE))

    k32[0] = jnp.zeros((TOK, PIECE), F32)
    v32[0] = jnp.zeros((TOK, PIECE), F32)

    pl.semaphore_wait(barrier, n_tp - 1 + n_zc - 1 + n_y - 1)

    meta_copies, k_copies, v_copies = [], [], []
    for k in range(1, n_tp):
        meta_copies.append(
            remote(meta.at[tp], meta.at[tp], meta_send.at[k], meta_recv.at[k], tp_dev(k))
        )
    for k in range(1, n_tp):
        k_copies.append(
            remote(keys_ref.at[:, columns(tp_at(k))], kp.at[tp], kp_send.at[k], kp_recv.at[k], tp_dev(k))
        )
    for k in range(1, n_tp):
        v_copies.append(
            remote(
                values_ref.at[:, columns(tp_at(k))], vp.at[tp], vp_send.at[k], vp_recv.at[k], tp_dev(k)
            )
        )

    for copy in meta_copies:
        copy.wait_recv()
    row_meta = meta[0]
    for t in range(1, n_tp):
        row_meta = jnp.maximum(row_meta, meta[t])
    src_v[...] = row_meta
    to_scalar = pltpu.make_async_copy(src_v, src_s, local_sem.at[2])
    to_scalar.start()
    code_columns = [
        jnp.transpose(jnp.broadcast_to(meta[t][0:1, :].astype(F32), (D, D)))[:tokens, :] for t in range(n_tp)
    ]

    own_k.wait()
    for copy in k_copies:
        copy.wait_recv()
    tops = []
    for h in range(LOCAL_HEADS):
        q_rows = q_head(h)
        top = jnp.full((1, ROWS), NEGATIVE, F32)
        for t in range(n_tp):
            dots = lax.dot_general(
                kp[t, :, pl.ds(h * D, D)], q_rows, NT, preferred_element_type=F32
            )
            masked = jnp.where(code_columns[t] == row_code, dots * SCALE, NEGATIVE)
            scores[h, pl.ds(t * tokens, tokens), :] = masked
            top = jnp.maximum(top, jnp.max(masked, axis=0, keepdims=True))
        tops.append(top)
    mx[0] = jnp.concatenate(tops + [row_meta[2:3, :].astype(F32), jnp.zeros((5, D), F32)], axis=0)
    mx_copies = [
        remote(mx.at[0], mx.at[k], mx_send.at[k], mx_recv.at[k], zc_dev(k)) for k in range(1, n_zc)
    ]

    def block_tile(ref, index):
        block = ref[index]
        return jnp.concatenate([block[:, :D], block[:, D:]], axis=0).astype(BF16)

    def source_of(k, j):
        return src_s[1, y_at(j) * n_zc + zc_at(k)]

    for t in range(n_tp):
        k32[pl.ds(1 + t * own_blocks, own_blocks)] = kp[t].astype(F32).reshape(own_blocks, TOK, PIECE)
    to_scalar.wait()

    k1_copies = []
    for k in list(range(1, n_zc)) + [0]:
        for j in range(n_y):
            tile = block_tile(k32, source_of(k, j))
            if k == 0:
                kb[0, j] = tile
            else:
                ka[k, j] = tile
        if k > 0:
            k1_copies.append(remote(ka.at[k], kb.at[k], k1_send.at[k], k1_recv.at[k], zc_dev(k)))

    own_v.wait()
    for copy in v_copies:
        copy.wait_recv()
    for t in range(n_tp):
        v32[pl.ds(1 + t * own_blocks, own_blocks)] = vp[t].astype(F32).reshape(own_blocks, TOK, PIECE)
    v1_copies = []
    for j in list(range(1, n_y)) + [0]:
        for k in range(n_zc):
            tile = block_tile(v32, source_of(k, j))
            if j == 0:
                vb[0, k] = tile
            else:
                va[j, k] = tile
        if j > 0:
            v1_copies.append(remote(va.at[j], vb.at[j], v1_send.at[j], v1_recv.at[j], y_dev(j)))

    for copy in mx_copies:
        copy.wait_recv()
    tile_max = mx[0]
    for k in range(1, n_zc):
        tile_max = jnp.maximum(tile_max, mx[k])
    for k in range(n_zc):
        my_buf[0, pl.ds(k, 1), :] = mx[k, pl.ds(2, 1), :]
    my_buf[0, pl.ds(n_zc, 8), :] = tile_max
    my_copies = [
        remote(my_buf.at[0], my_buf.at[j], my_send.at[j], my_recv.at[j], y_dev(j))
        for j in range(1, n_y)
    ]
    for copy in my_copies:
        copy.wait_recv()
    all_max = my_buf[0, pl.ds(n_zc, 8), :]
    for j in range(1, n_y):
        all_max = jnp.maximum(all_max, my_buf[j, pl.ds(n_zc, 8), :])

    chunk = D // n_zc
    row_tops = []
    for h in range(LOCAL_HEADS):
        row_top = jnp.maximum(
            all_max[h : h + 1, :], jnp.max(fresh_scores[h], axis=0, keepdims=True)
        )
        row_tops.append(row_top)
        total = jnp.zeros((1, ROWS), F32)
        number = jnp.zeros((D, ROWS), F32)
        for t in range(n_tp):
            weights = jnp.exp(scores[h, pl.ds(t * tokens, tokens), :] - row_top)
            total = total + jnp.sum(weights, axis=0, keepdims=True)
            number = number + lax.dot_general(
                vp[t, :, pl.ds(h * D, D)], weights.astype(BF16), TN, preferred_element_type=F32
            )
        for p in range(n_zc):
            rs_src[p, pl.ds(h * chunk, chunk), :] = number[p * chunk : (p + 1) * chunk, :]
            rs_src[p, pl.ds(LOCAL_HEADS * chunk + h, 1), :] = total
    rs_copies = []
    for k in range(1, n_zc):
        rs_copies.append(
            remote(rs_src.at[zc_at(k)], rs_buf.at[mzc], rs_send.at[k], rs_recv.at[k], zc_dev(k))
        )
    rs_buf[mzc] = rs_src[mzc]

    fresh_totals = []
    for h in range(LOCAL_HEADS):
        weights = jnp.exp(fresh_scores[h] - row_tops[h])
        fresh_totals.append(jnp.sum(weights, axis=0, keepdims=True))
        number = lax.dot_general(
            fresh_v_ref[:, pl.ds(h * D, D)], weights.astype(BF16), TN, preferred_element_type=F32
        )
        for p in range(n_zc):
            fresh_num[p, pl.ds(h * chunk, chunk), :] = number[p * chunk : (p + 1) * chunk, :]

    column = []
    for j in range(n_y):
        lists = my_buf[j, pl.ds(0, n_zc), :]
        wide = lax.broadcasted_iota(jnp.int32, (n_zc, D), 1)
        picked = jnp.sum(jnp.where(wide == me, lists, 0.0), axis=1, keepdims=True)
        index = lax.broadcasted_iota(jnp.int32, (n_zc, D), 0) + (j * n_zc + 1)
        found = jnp.where(picked == (wide + 1).astype(F32), index, 0)
        column.append(jnp.sum(found, axis=0, keepdims=True))
    arrival = column[0]
    for j in range(1, n_y):
        arrival = arrival + column[j]
    arrival_ref[...] = jnp.broadcast_to(arrival, (8, D))

    k2_copies = []
    for copy in k1_copies:
        copy.wait_recv()
    for j in range(1, n_y):
        k2_copies.append(remote(kb.at[:, j], kc.at[j], k2_send.at[j], k2_recv.at[j], y_dev(j)))
    own_k2 = pltpu.make_async_copy(kb.at[:, 0], kc.at[0], local_sem.at[3])
    own_k2.start()

    for copy in rs_copies:
        copy.wait_recv()
    part = rs_buf[0]
    for p in range(1, n_zc):
        part = part + rs_buf[p]
    yy_buf[my] = part
    yy_copies = [
        remote(yy_buf.at[my], yy_buf.at[my], yy_send.at[j], yy_recv.at[j], y_dev(j))
        for j in range(1, n_y)
    ]

    v2_copies = []
    for copy in v1_copies:
        copy.wait_recv()
    for k in range(1, n_zc):
        v2_copies.append(remote(vb.at[:, k], vc.at[:, k], v2_send.at[k], v2_recv.at[k], zc_dev(k)))
    own_v2 = pltpu.make_async_copy(vb.at[:, 0], vc.at[:, 0], local_sem.at[4])
    own_v2.start()

    for copy in yy_copies:
        copy.wait_recv()
    whole = yy_buf[0]
    for j in range(1, n_y):
        whole = whole + yy_buf[j]
    norms = []
    for h in range(LOCAL_HEADS):
        total = whole[LOCAL_HEADS * chunk + h : LOCAL_HEADS * chunk + h + 1, :] + fresh_totals[h]
        number = whole[h * chunk : (h + 1) * chunk, :] + fresh_num[mzc, pl.ds(h * chunk, chunk), :]
        ag_buf[mzc, pl.ds(h * chunk, chunk), :] = number / total
        norms.append(row_tops[h] + jnp.log(total))
    norm_ref[...] = jnp.concatenate(norms + [jnp.zeros((6, ROWS), F32)], axis=0)
    ag_copies = [
        remote(ag_buf.at[mzc], ag_buf.at[mzc], ag_send.at[k], ag_recv.at[k], zc_dev(k))
        for k in range(1, n_zc)
    ]
    for copy in ag_copies:
        copy.wait_recv()
    for h in range(LOCAL_HEADS):
        by_entry = jnp.concatenate(
            [ag_buf[p, pl.ds(h * chunk, chunk), :] for p in range(n_zc)], axis=0
        )
        by_row = jnp.transpose(by_entry)
        for g in range(GROUP):
            attended_ref[:, pl.ds((h * GROUP + g) * D, D)] = by_row[g * SR : (g + 1) * SR, :]

    for copy in k2_copies + v2_copies:
        copy.wait_recv()
    own_k2.wait()
    own_v2.wait()
    for copy in (
        meta_copies
        + k_copies
        + v_copies
        + mx_copies
        + my_copies
        + k1_copies
        + v1_copies
        + k2_copies
        + v2_copies
        + rs_copies
        + yy_copies
        + ag_copies
    ):
        copy.wait_send()


def place_kernel(slot_count, arrival_ref, k_ref, v_ref, out_k_ref, out_v_ref):
    def place(s, carry):
        index = arrival_ref[s]
        at = jnp.maximum(index - 1, 0)
        there = index > 0
        for ref, out in ((k_ref, out_k_ref), (v_ref, out_v_ref)):
            tile = ref[at].astype(F32)
            wide = jnp.concatenate([tile[:TOK, :], tile[TOK:, :]], axis=1)
            out[s] = jnp.where(there, wide, 0.0).astype(BF16)
        return carry

    lax.fori_loop(0, slot_count, place, 0, unroll=4)


def on_device(
    n_y,
    n_zc,
    prefilled_block_keys,
    prefilled_block_values,
    queries,
    step_token_keys,
    step_token_values,
    lengths,
    block_request,
    block_number,
    owner_rank,
    owner_slot,
    group_first,
):
    n_tp = lax.axis_size("tp")
    own_blocks, _, full_width = prefilled_block_keys.shape
    row_blocks = own_blocks * n_tp
    tokens = own_blocks * TOK
    slot_count = 2 * row_blocks
    n_sp = n_y * n_zc
    chunk = D // n_zc
    rs_rows = LOCAL_HEADS * chunk + 8
    smem = pl.BlockSpec(memory_space=pltpu.SMEM)
    vmem = pl.BlockSpec(memory_space=pltpu.VMEM)
    hbm = pl.BlockSpec(memory_space=pl.ANY)
    dma = pltpu.SemaphoreType.DMA
    attended, norms, arrival, kc, vc = pl.pallas_call(
        functools.partial(exchange_kernel, n_y, n_zc, n_tp, own_blocks),
        out_shape=(
            jax.ShapeDtypeStruct((SR, GROUP * PIECE), F32),
            jax.ShapeDtypeStruct((8, ROWS), F32),
            jax.ShapeDtypeStruct((8, D), jnp.int32),
            jax.ShapeDtypeStruct((n_y, n_zc, 2 * TOK, D), BF16),
            jax.ShapeDtypeStruct((n_y, n_zc, 2 * TOK, D), BF16),
        ),
        in_specs=[smem] * 6 + [vmem] * 3 + [hbm] * 2,
        out_specs=(vmem,) * 5,
        scratch_shapes=[
            pltpu.VMEM((n_tp, 8, D), jnp.int32),
            pltpu.VMEM((n_tp, tokens, PIECE), BF16),
            pltpu.VMEM((n_tp, tokens, PIECE), BF16),
            pltpu.VMEM((row_blocks + 1, TOK, PIECE), F32),
            pltpu.VMEM((row_blocks + 1, TOK, PIECE), F32),
            pltpu.VMEM((8, D), jnp.int32),
            pltpu.SMEM((8, D), jnp.int32),
            pltpu.VMEM((LOCAL_HEADS, n_tp * tokens, ROWS), F32),
            pltpu.VMEM((n_zc, n_y, 2 * TOK, D), BF16),
            pltpu.VMEM((n_zc, n_y, 2 * TOK, D), BF16),
            pltpu.VMEM((n_y, n_zc, 2 * TOK, D), BF16),
            pltpu.VMEM((n_y, n_zc, 2 * TOK, D), BF16),
            pltpu.VMEM((n_zc, 8, D), F32),
            pltpu.VMEM((8, D), F32),
            pltpu.VMEM((n_y, n_zc + 8, D), F32),
            pltpu.VMEM((n_zc, LOCAL_HEADS * chunk, ROWS), F32),
            pltpu.VMEM((n_zc, rs_rows, ROWS), F32),
            pltpu.VMEM((n_zc, rs_rows, ROWS), F32),
            pltpu.VMEM((n_y, rs_rows, ROWS), F32),
            pltpu.VMEM((n_zc, LOCAL_HEADS * chunk, ROWS), F32),
            dma((5,)),
        ]
        + [dma((n_tp,))] * 6
        + [dma((n_zc,))] * 2
        + [dma((n_y,))] * 2
        + [dma((n_zc,))] * 2
        + [dma((n_y,))] * 2
        + [dma((n_y,))] * 2
        + [dma((n_zc,))] * 2
        + [dma((n_zc,))] * 2
        + [dma((n_y,))] * 2
        + [dma((n_zc,))] * 2,
        compiler_params=pltpu.CompilerParams(
            collective_id=0, has_side_effects=True, vmem_limit_bytes=40 * 2**20
        ),
        name="exchange",
    )(
        block_request,
        block_number,
        owner_rank,
        owner_slot,
        lengths,
        group_first,
        queries.reshape(SR, GROUP * PIECE),
        step_token_keys.reshape(SR, PIECE),
        step_token_values.reshape(SR, PIECE),
        prefilled_block_keys.reshape(tokens, full_width),
        prefilled_block_values.reshape(tokens, full_width),
    )
    slot_shape = jax.ShapeDtypeStruct((slot_count, TOK, PIECE), BF16)
    owner_slot_keys, owner_slot_values = pl.pallas_call(
        functools.partial(place_kernel, slot_count),
        out_shape=(slot_shape, slot_shape),
        in_specs=[smem, vmem, vmem],
        out_specs=(vmem, vmem),
        compiler_params=pltpu.CompilerParams(vmem_limit_bytes=16 * 2**20),
        name="place",
    )(
        arrival[0],
        kc.reshape(n_sp, 2 * TOK, D),
        vc.reshape(n_sp, 2 * TOK, D),
    )
    log_norm = (
        norms[:LOCAL_HEADS]
        .reshape(LOCAL_HEADS, GROUP, STEPS, REQUESTS)
        .transpose(2, 3, 0, 1)
        .reshape(STEPS, REQUESTS, LOCAL_HEADS * GROUP)
    )
    return (
        attended.reshape(STEPS, REQUESTS, GROUP * PIECE),
        log_norm,
        owner_slot_keys,
        owner_slot_values,
    )


def solution(mesh):
    sp = mesh.shape["sp"]
    n_y = max(2, sp // 16)
    return jax.shard_map(
        functools.partial(on_device, n_y, sp // n_y),
        mesh=mesh,
        in_specs=(
            P(("sp", "tp"), None, None),
            P(("sp", "tp"), None, None),
            P(None, None, "tp"),
            P(None, None, "tp"),
            P(None, None, "tp"),
            P(),
            P(("sp", "tp")),
            P(("sp", "tp")),
            P(("sp", "tp")),
            P(("sp", "tp")),
            P(),
        ),
        out_specs=(
            P(None, None, "tp"),
            P(None, None, "tp"),
            P("sp", None, "tp"),
            P("sp", None, "tp"),
        ),
        check_vma=False,
    )
```

time: 1390 us -> 76.2 us (0.05)
  blocking collectives: 1110 us -> 0 us
  waiting for transfers between devices: 214 us -> 0 us
  Pallas kernels: 0 us -> 70.2 us
  starting transfers between devices: 26.9 us -> 0 us
    psum x1 -> x0, blocking collectives: 491 us -> none  [attend(): numerator, weight_sum = lax.psum((numerator, weight_sum), 'sp')]
    pmax x1 -> x0, blocking collectives: 487 us -> none  [attend(): row_top = lax.pmax(local_top, 'sp')]
    psum x1 -> x0, waiting for transfers between devices: 179 us -> none  [attend(): numerator, weight_sum = lax.psum((numerator, weight_sum), 'sp')]
    all_gather x1 -> x0, blocking collectives: 132 us -> none  [on_device(): lax.all_gather(block_tables, ('sp', 'tp'), axis=0, tiled=True)]
    pallas_call x0 -> x2, Pallas kernels: none -> 70.2 us  [the longest x1 68.1 us: on_device(): pl.pallas_call(functools.partial(exchange_kernel, n_y, n_zc, n_tp, own_bl...]
    all_to_all x4 -> x0, waiting for transfers between devices: 34.7 us -> none  [the longest x1 18 us: on_device(): lax.all_to_all(send_values, 'sp', split_axis=0, concat_axis=0, tiled=True)]
    all_to_all x4 -> x0, starting transfers between devices: 26.6 us -> none  [the longest x1 11.1 us: on_device(): lax.all_to_all(send_keys, 'sp', split_axis=0, concat_axis=0, tiled=True)]
  transfers between devices with their start and end apart: 5 -> 0, of which waited for: 4 -> 0; matrix products, arithmetic and copies ran while one was open for 1% -> 0% of each run, Pallas kernels for 0% -> 0%
where the time goes in v1:
time: 76.2 us; the launch traced here: 76 us
  Pallas kernels  70.2 us (92%)
  local copies, waits for them, and re-layouts  5.06 us (7%)
    pallas_call x1, Pallas kernels, on_device(): pl.pallas_call(functools.partial(exchange_kernel, n_y, n_zc, n_tp, own_bl...  68.1 us
    unnamed x19, local copies, waits for them, and re-layouts  2.64 us
    pallas_call x1, Pallas kernels, on_device(): pl.pallas_call(functools.partial(place_kernel, slot_count), out_shape=(sl...  2.08 us

profile of v1, /device:TPU:1, one launch (start us, length us, event | category | flops | bytes accessed | tf_op | source)
XLA Modules:
  0.0 76.0 jit_solution(5424520794723913706)
XLA Ops:
  0.6 0.0 copy-start.8
  0.6 0.7 reshape.39.fresh_k_ref
  1.4 0.0 copy-done.8
  1.4 0.0 copy-start.2
  1.4 0.0 copy-start.3
  1.4 0.0 copy-start.4
  1.4 0.0 copy-start.5
  1.4 0.0 copy-start.6
  1.4 0.0 copy-start.7
  1.4 0.9 %reshape.38.q_ref = bf16[16,2048]{1,0:T(8,128)(2,1)S(1)} reshape(bf16[4,4,2048]{2,1,0:T(4,128)(2,1)} %param.13) | data formatting | bytes 131072 | tf_op jit(solution)/shard_map/reshape | solution.py:507
  2.3 0.0 copy-done.2
  2.3 0.0 copy-done.3
  2.3 0.0 copy-done.4
  2.4 0.0 copy-done.5
  2.4 0.0 copy-done.6
  2.4 0.0 copy-done.7
  2.4 0.0 copy-start
  2.4 0.9 %copy-done = bf16[16,8,1024]{2,1,0:T(8,128)(2,1)S(1)} copy-done((bf16[16,8,1024]{2,1,0:T(8,128)(2,1)S(1)}, bf16[16,8,1024]{2,1,0:T(8,128)(2,1)}, u32[]{:S(2)}) %copy-start) | copy-done | bytes 262168
  3.3 0.0 copy-start.1
  3.3 0.9 %copy-done.1 = bf16[16,8,1024]{2,1,0:T(8,128)(2,1)S(1)} copy-done((bf16[16,8,1024]{2,1,0:T(8,128)(2,1)S(1)}, bf16[16,8,1024]{2,1,0:T(8,128)(2,1)}, u32[]{:S(2)}) %copy-start.1) | copy-done | bytes 262168
  4.3 68.1 %exchange.1 = (f32[16,2048]{1,0:T(8,128)S(1)}, f32[8,128]{1,0:T(8,128)S(1)}, s32[8,128]{1,0:T(8,128)S(1)}, bf16[8,16,16,128]{3,2,1,0:T(8,128)(2,1)S(1)}, bf16[8,16,16,128]{3,2,1,0:T(8,128)(2,1)S(1)}) custom-call(s32[16]{0:T(128)S(1)} %copy-done.2, s32[16]{0:T(128)S(1)} %copy-done.3, s32[16]{0:T(128)S(1)} %copy-done.4, s32[16]{0:T(128)S(1)} %copy-done.5, ...), custom_call_target="tpu_custom_call" | custom-call | tf_op jit(solution)/shard_map/exchange/pallas_call | solution.py:452
  72.4 0.7 reshape.43
  73.1 2.1 %place.1 = (bf16[128,8,256]{2,1,0:T(8,128)(2,1)}, bf16[128,8,256]{2,1,0:T(8,128)(2,1)}) custom-call(s32[128]{0:T(128)S(1)} %slice_bitcast_fusion.arrival_ref, bf16[128,16,128]{2,1,0:T(8,128)(2,1)S(1)} %bitcast.9, bf16[128,16,128]{2,1,0:T(8,128)(2,1)S(1)} %bitcast.10), custom_call_target="tpu_custom_call" | custom-call | tf_op jit(solution)/shard_map/place/pallas_call | solution.py:514
  75.2 0.1 reshape.44
  75.3 0.7 copy.16
  (3 shorter events, 0.0 us)
Async XLA Ops:
  0.6 0.7 copy-start.8
  1.4 1.0 %copy-start.2 = (s32[16]{0:T(128)S(1)}, s32[16]{0:T(128)}, u32[]{:S(2)}) copy-start(s32[16]{0:T(128)} %request_ref.1) | copy-start | bytes 196
  1.4 1.0 %copy-start.3 = (s32[16]{0:T(128)S(1)}, s32[16]{0:T(128)}, u32[]{:S(2)}) copy-start(s32[16]{0:T(128)} %number_ref.1) | copy-start | bytes 196
  1.4 1.0 %copy-start.4 = (s32[16]{0:T(128)S(1)}, s32[16]{0:T(128)}, u32[]{:S(2)}) copy-start(s32[16]{0:T(128)} %rank_ref.1) | copy-start | bytes 196
  1.4 1.0 %copy-start.5 = (s32[16]{0:T(128)S(1)}, s32[16]{0:T(128)}, u32[]{:S(2)}) copy-start(s32[16]{0:T(128)} %slot_ref.1) | copy-start | bytes 196
  1.4 1.0 %copy-start.6 = (s32[4]{0:T(128)S(1)}, s32[4]{0:T(128)}, u32[]{:S(2)}) copy-start(s32[4]{0:T(128)} %lengths_ref.1) | copy-start | bytes 52
  1.4 0.9 %copy-start.7 = (s32[4]{0:T(128)S(1)}, s32[4]{0:T(128)}, u32[]{:S(2)}) copy-start(s32[4]{0:T(128)} %first_ref.1) | copy-start | bytes 52
  2.4 1.0 %copy-start = (bf16[16,8,1024]{2,1,0:T(8,128)(2,1)S(1)}, bf16[16,8,1024]{2,1,0:T(8,128)(2,1)}, u32[]{:S(2)}) copy-start(bf16[16,8,1024]{2,1,0:T(8,128)(2,1)} %param.11) | copy-start | bytes 786436
  3.3 0.9 %copy-start.1 = (bf16[16,8,1024]{2,1,0:T(8,128)(2,1)S(1)}, bf16[16,8,1024]{2,1,0:T(8,128)(2,1)}, u32[]{:S(2)}) copy-start(bf16[16,8,1024]{2,1,0:T(8,128)(2,1)} %param.12) | copy-start | bytes 786436

commit v2 on v1

v2 whole, which is shorter than its diff:
```python
import functools
import math

import jax
import jax.numpy as jnp
from jax import lax
from jax.experimental import pallas as pl
from jax.experimental.pallas import tpu as pltpu
from jax.sharding import PartitionSpec as P

D = 128
TOK = 8
STEPS = 4
REQUESTS = 4
SR = STEPS * REQUESTS
GROUP = 8
ROWS = GROUP * SR
LOCAL_HEADS = 2
PIECE = LOCAL_HEADS * D
NEGATIVE = -1e30
SCALE = 1.0 / math.sqrt(D)
MESH = pl.DeviceIdType.MESH
F32 = jnp.float32
BF16 = jnp.bfloat16
NT = (((1,), (1,)), ((), ()))
TN = (((0,), (0,)), ((), ()))


def exchange_kernel(
    n_y,
    n_zc,
    n_tp,
    own_blocks,
    request_ref,
    number_ref,
    rank_ref,
    slot_ref,
    lengths_ref,
    first_ref,
    q_ref,
    fresh_k_ref,
    fresh_v_ref,
    keys_ref,
    values_ref,
    attended_ref,
    norm_ref,
    arrival_ref,
    kc,
    vc,
    meta,
    kp,
    vp,
    k32,
    v32,
    src_v,
    src_s,
    scores,
    ka,
    kb,
    va,
    vb,
    qs,
    fresh_ks,
    fresh_vs,
    sl,
    sy,
    su,
    sv,
    mx,
    my_buf,
    fresh_num,
    rs_src,
    rs_buf,
    yy_buf,
    ag_buf,
    local_sem,
    meta_send,
    meta_recv,
    kp_send,
    kp_recv,
    vp_send,
    vp_recv,
    sl_send,
    sl_recv,
    sy_send,
    sy_recv,
    su_send,
    su_recv,
    sv_send,
    sv_recv,
    mx_send,
    mx_recv,
    my_send,
    my_recv,
    z_send,
    z_recv,
    y_send,
    y_recv,
    rs_send,
    rs_recv,
    yy_send,
    yy_recv,
    ag_send,
    ag_recv,
):
    me = lax.axis_index("sp")
    tp = lax.axis_index("tp")
    my = me // n_zc
    mzc = lax.rem(me, n_zc)
    tokens = own_blocks * TOK

    def zc_at(k):
        return lax.rem(mzc + k, n_zc)

    def y_at(j):
        return lax.rem(my + j, n_y)

    def tp_at(k):
        return lax.rem(tp + k, n_tp)

    z_order = sorted(range(1, n_zc), key=lambda k: -min(k, n_zc - k))
    y_order = sorted(range(1, n_y), key=lambda j: -min(j, n_y - j))
    odd_order = [(j - 1) // 2 for j in y_order if j % 2]
    even_order = [j // 2 for j in y_order if j % 2 == 0]

    def zc_dev(k):
        return (my * n_zc + zc_at(k), tp)

    def y_dev(j):
        return (y_at(j) * n_zc + mzc, tp)

    def tp_dev(k):
        return (me, tp_at(k))

    def remote(src, dst, send, recv, dev):
        copy = pltpu.make_async_remote_copy(
            src_ref=src, dst_ref=dst, send_sem=send, recv_sem=recv, device_id=dev, device_id_type=MESH
        )
        copy.start()
        return copy

    barrier = pltpu.get_barrier_semaphore()
    for k in range(1, n_tp):
        pl.semaphore_signal(barrier, inc=1, device_id=tp_dev(k), device_id_type=MESH)
    for k in range(1, n_zc):
        pl.semaphore_signal(barrier, inc=1, device_id=zc_dev(k), device_id_type=MESH)
    for j in range(1, n_y):
        pl.semaphore_signal(barrier, inc=1, device_id=y_dev(j), device_id_type=MESH)

    def columns(t):
        return pl.ds(pl.multiple_of(t * PIECE, PIECE), PIECE)

    def rows_of(t):
        return pl.ds(pl.multiple_of(t * tokens, tokens), tokens)

    own_k = pltpu.make_async_copy(keys_ref.at[:, columns(tp)], kp.at[rows_of(tp)], local_sem.at[0])
    own_v = pltpu.make_async_copy(values_ref.at[:, columns(tp)], vp.at[rows_of(tp)], local_sem.at[1])
    own_k.start()
    own_v.start()

    lane = lax.broadcasted_iota(jnp.int32, (1, D), 1)
    codes = jnp.full((1, D), REQUESTS, jnp.int32)
    sources = jnp.zeros((1, D), jnp.int32)
    slots = jnp.zeros((1, D), jnp.int32)
    for b in range(own_blocks):
        request = request_ref[b]
        owner = first_ref[request] + rank_ref[b]
        place = number_ref[b] * TOK + (lane - b * TOK)
        mine = (lane >= b * TOK) & (lane < (b + 1) * TOK) & (place < lengths_ref[request])
        codes = jnp.where(mine, request, codes)
        hit = lane == owner
        sources = jnp.where(hit, tp * own_blocks + b + 1, sources)
        slots = jnp.where(hit, slot_ref[b] + 1, slots)
    own_meta = jnp.concatenate(
        [codes, sources, slots, jnp.zeros((5, D), jnp.int32)], axis=0
    )
    meta[tp] = own_meta

    row_lane = lax.broadcasted_iota(jnp.int32, (1, ROWS), 1)
    row_request = lax.rem(row_lane, REQUESTS)
    row_step = lax.rem(row_lane, SR) // REQUESTS
    row_code = row_request.astype(F32)

    def stack_steps(ref, out):
        out[...] = jnp.concatenate([ref[s].astype(F32) for s in range(STEPS)], axis=0).astype(BF16)

    stack_steps(q_ref, qs)
    stack_steps(fresh_k_ref, fresh_ks)
    stack_steps(fresh_v_ref, fresh_vs)

    def q_head(h):
        return jnp.concatenate(
            [qs[:, pl.ds((h * GROUP + g) * D, D)] for g in range(GROUP)], axis=0
        )

    fresh_row = lax.broadcasted_iota(jnp.int32, (SR, ROWS), 0)
    fresh_ok = (lax.rem(fresh_row, REQUESTS) == row_request) & (fresh_row // REQUESTS <= row_step)
    fresh_scores = []
    for h in range(LOCAL_HEADS):
        dots = lax.dot_general(
            fresh_ks[:, pl.ds(h * D, D)], q_head(h), NT, preferred_element_type=F32
        )
        fresh_scores.append(jnp.where(fresh_ok, dots * SCALE, NEGATIVE))

    k32[0] = jnp.zeros((TOK, PIECE), F32)
    v32[0] = jnp.zeros((TOK, PIECE), F32)

    pl.semaphore_wait(barrier, n_tp - 1 + n_zc - 1 + n_y - 1)

    meta_copies, k_copies, v_copies = [], [], []
    for k in range(1, n_tp):
        meta_copies.append(
            remote(meta.at[tp], meta.at[tp], meta_send.at[k], meta_recv.at[k], tp_dev(k))
        )
    for k in range(1, n_tp):
        k_copies.append(
            remote(keys_ref.at[:, columns(tp_at(k))], kp.at[rows_of(tp)], kp_send.at[k], kp_recv.at[k], tp_dev(k))
        )
    for k in range(1, n_tp):
        v_copies.append(
            remote(
                values_ref.at[:, columns(tp_at(k))], vp.at[rows_of(tp)], vp_send.at[k], vp_recv.at[k], tp_dev(k)
            )
        )

    for copy in meta_copies:
        copy.wait_recv()
    row_meta = meta[0]
    for t in range(1, n_tp):
        row_meta = jnp.maximum(row_meta, meta[t])
    src_v[...] = row_meta
    to_scalar = pltpu.make_async_copy(src_v, src_s, local_sem.at[2])
    to_scalar.start()
    sl[0] = row_meta[2:3, :]
    sl_copies = [
        remote(sl.at[0], sl.at[k], sl_send.at[k], sl_recv.at[k], zc_dev(k)) for k in z_order
    ]
    code_column = jnp.concatenate(
        [
            jnp.transpose(jnp.broadcast_to(meta[t][0:1, :].astype(F32), (D, D)))[:tokens, :]
            for t in range(n_tp)
        ],
        axis=0,
    )
    allowed = code_column == row_code

    own_k.wait()
    for copy in k_copies:
        copy.wait_recv()
    for h in range(LOCAL_HEADS):
        dots = lax.dot_general(kp[:, pl.ds(h * D, D)], q_head(h), NT, preferred_element_type=F32)
        masked = jnp.where(allowed, dots * SCALE, NEGATIVE)
        scores[h] = masked
        mx[0, pl.ds(h, 1), :] = jnp.max(masked, axis=0, keepdims=True)
    mx_copies = [
        remote(mx.at[0], mx.at[k], mx_send.at[k], mx_recv.at[k], zc_dev(k)) for k in z_order
    ]

    def block_tile(ref, index):
        block = ref[index]
        return jnp.concatenate([block[:, :D], block[:, D:]], axis=0).astype(BF16)

    half = n_y // 2
    y_starts = [y_at(j) * n_zc for j in range(n_y)]
    zc_places = [zc_at(k) for k in range(n_zc)]

    def source_of(k, j):
        return src_s[1, y_starts[j] + zc_places[k]]

    def gather_z(x, staged, k):
        for i in range(half):
            tile = block_tile(staged, source_of(k, 2 * i))
            if k == 0:
                kb[x, 0, i] = tile
            else:
                ka[x, k, i] = tile

    def gather_y(x, staged, i):
        for k in range(n_zc):
            va[x, i, k] = block_tile(staged, source_of(k, 2 * i + 1))

    def z_first(x, k):
        return remote(ka.at[x, k], kb.at[x, k], z_send.at[x, 0, k], z_recv.at[x, 0, k], zc_dev(k))

    def y_first(x, i):
        return remote(
            va.at[x, i], vb.at[x, i], y_send.at[x, 0, i], y_recv.at[x, 0, i], y_dev(2 * i + 1)
        )

    def y_second(x, out, i):
        return remote(
            kb.at[x, :, i], out.at[0, i], y_send.at[x, 1, i], y_recv.at[x, 1, i], y_dev(2 * i)
        )

    def z_second(x, out, k):
        return remote(
            vb.at[x, :, k], out.at[1, :, k], z_send.at[x, 1, k], z_recv.at[x, 1, k], zc_dev(k)
        )

    local_copies = []

    def keep(src, dst):
        copy = pltpu.make_async_copy(src, dst, local_sem.at[3 + len(local_copies)])
        copy.start()
        local_copies.append(copy)

    k32[pl.ds(1, n_tp * own_blocks)] = kp[...].astype(F32).reshape(n_tp * own_blocks, TOK, PIECE)
    to_scalar.wait()

    kz1, ky1, vz1, vy1 = [], [], [], []
    per = -(-(n_zc - 1) // half)
    for n, i in enumerate(odd_order):
        gather_y(0, k32, i)
        ky1.append(y_first(0, i))
        for k in z_order[n * per : (n + 1) * per]:
            gather_z(0, k32, k)
            kz1.append(z_first(0, k))
    gather_z(0, k32, 0)

    own_v.wait()
    for copy in v_copies:
        copy.wait_recv()
    v32[pl.ds(1, n_tp * own_blocks)] = vp[...].astype(F32).reshape(n_tp * own_blocks, TOK, PIECE)
    for k in z_order:
        gather_z(1, v32, k)
        vz1.append(z_first(1, k))
    gather_z(1, v32, 0)
    for i in range(half):
        gather_y(1, v32, i)

    for copy in mx_copies:
        copy.wait_recv()
    row_max = mx[0]
    for k in range(1, n_zc):
        row_max = jnp.maximum(row_max, mx[k])
    my_buf[0] = row_max
    my_copies = [
        remote(my_buf.at[0], my_buf.at[j], my_send.at[j], my_recv.at[j], y_dev(j)) for j in y_order
    ]
    for copy in sl_copies:
        copy.wait_recv()
    for k in range(n_zc):
        sy[0, pl.ds(k, 1), :] = sl[k]
    sy_copies = [
        remote(sy.at[0], sy.at[j], sy_send.at[j], sy_recv.at[j], y_dev(j)) for j in y_order
    ]
    for i in odd_order:
        vy1.append(y_first(1, i))
    for copy in kz1:
        copy.wait_recv()
    ky2 = [y_second(0, kc, i) for i in even_order]
    keep(kb.at[0, :, 0], kc.at[0, 0])
    for copy in my_copies:
        copy.wait_recv()
    all_max = my_buf[0]
    for j in range(1, n_y):
        all_max = jnp.maximum(all_max, my_buf[j])

    chunk = D // n_zc
    row_tops = []
    for h in range(LOCAL_HEADS):
        row_top = jnp.maximum(
            all_max[h : h + 1, :], jnp.max(fresh_scores[h], axis=0, keepdims=True)
        )
        row_tops.append(row_top)
        weights = jnp.exp(scores[h] - row_top)
        su[mzc, pl.ds(h, 1), :] = jnp.sum(weights, axis=0, keepdims=True)
        number = lax.dot_general(
            vp[:, pl.ds(h * D, D)], weights.astype(BF16), TN, preferred_element_type=F32
        )
        for p in range(n_zc):
            rs_src[p, pl.ds(h * chunk, chunk), :] = number[p * chunk : (p + 1) * chunk, :]
    rs_copies = [
        remote(rs_src.at[zc_at(k)], rs_buf.at[mzc], rs_send.at[k], rs_recv.at[k], zc_dev(k))
        for k in z_order
    ]
    su_copies = [
        remote(su.at[mzc], su.at[mzc], su_send.at[k], su_recv.at[k], zc_dev(k)) for k in z_order
    ]
    rs_buf[mzc] = rs_src[mzc]

    for copy in ky1:
        copy.wait_recv()
    kz2 = [z_second(0, kc, k) for k in z_order]
    keep(vb.at[0, :, 0], kc.at[1, :, 0])

    fresh_totals = []
    for h in range(LOCAL_HEADS):
        weights = jnp.exp(fresh_scores[h] - row_tops[h])
        fresh_totals.append(jnp.sum(weights, axis=0, keepdims=True))
        number = lax.dot_general(
            fresh_vs[:, pl.ds(h * D, D)], weights.astype(BF16), TN, preferred_element_type=F32
        )
        for p in range(n_zc):
            fresh_num[p, pl.ds(h * chunk, chunk), :] = number[p * chunk : (p + 1) * chunk, :]

    for copy in sy_copies:
        copy.wait_recv()
    column = []
    for j in range(n_y):
        first_place = (j % 2) * half * n_zc + (j // 2) * n_zc + 1
        lists = sy[j]
        wide = lax.broadcasted_iota(jnp.int32, (n_zc, D), 1)
        picked = jnp.sum(jnp.where(wide == me, lists, 0), axis=1, keepdims=True)
        index = lax.broadcasted_iota(jnp.int32, (n_zc, D), 0) + first_place
        found = jnp.where(picked == wide + 1, index, 0)
        column.append(jnp.max(found, axis=0, keepdims=True))
    arrival = column[0]
    for j in range(1, n_y):
        arrival = jnp.maximum(arrival, column[j])
    arrival_ref[...] = jnp.broadcast_to(arrival, (8, D))

    for copy in rs_copies:
        copy.wait_recv()
    part = rs_buf[0]
    for p in range(1, n_zc):
        part = part + rs_buf[p]
    yy_buf[my] = part
    yy_copies = [
        remote(yy_buf.at[my], yy_buf.at[my], yy_send.at[j], yy_recv.at[j], y_dev(j)) for j in y_order
    ]
    for copy in su_copies:
        copy.wait_recv()
    part = su[0]
    for p in range(1, n_zc):
        part = part + su[p]
    sv[my] = part
    sv_copies = [
        remote(sv.at[my], sv.at[my], sv_send.at[j], sv_recv.at[j], y_dev(j)) for j in y_order
    ]

    for copy in vz1:
        copy.wait_recv()
    vy2 = [y_second(1, vc, i) for i in even_order]
    keep(kb.at[1, :, 0], vc.at[0, 0])
    for copy in vy1:
        copy.wait_recv()
    vz2 = [z_second(1, vc, k) for k in z_order[: n_zc // 2]]
    keep(vb.at[1, :, 0], vc.at[1, :, 0])

    for copy in yy_copies:
        copy.wait_recv()
    whole = yy_buf[0]
    for copy in sv_copies:
        copy.wait_recv()
    sums = sv[0]
    for j in range(1, n_y):
        whole = whole + yy_buf[j]
        sums = sums + sv[j]
    norms = []
    for h in range(LOCAL_HEADS):
        total = sums[h : h + 1, :] + fresh_totals[h]
        number = whole[h * chunk : (h + 1) * chunk, :] + fresh_num[mzc, pl.ds(h * chunk, chunk), :]
        ag_buf[mzc, pl.ds(h * chunk, chunk), :] = number / total
        norms.append(row_tops[h] + jnp.log(total))
    ag_copies = [
        remote(ag_buf.at[mzc], ag_buf.at[mzc], ag_send.at[k], ag_recv.at[k], zc_dev(k))
        for k in z_order
    ]
    vz2 += [z_second(1, vc, k) for k in z_order[n_zc // 2 :]]
    wide_lane = lax.broadcasted_iota(jnp.int32, (SR, D), 1)
    wide_row = lax.broadcasted_iota(jnp.int32, (SR, D), 0)
    by_head = jnp.zeros((SR, D), F32)
    for h in range(LOCAL_HEADS):
        for g in range(GROUP):
            picked = jnp.where(wide_lane == wide_row + g * SR, norms[h], 0.0)
            value = jnp.sum(picked, axis=1, keepdims=True)
            by_head = jnp.where(wide_lane == h * GROUP + g, value, by_head)
    norm_ref[...] = by_head
    for copy in ag_copies:
        copy.wait_recv()
    for h in range(LOCAL_HEADS):
        by_entry = jnp.concatenate(
            [ag_buf[p, pl.ds(h * chunk, chunk), :] for p in range(n_zc)], axis=0
        )
        by_row = jnp.transpose(by_entry)
        for g in range(GROUP):
            attended_ref[:, pl.ds((h * GROUP + g) * D, D)] = by_row[g * SR : (g + 1) * SR, :]

    for copy in kz2 + ky2 + vz2 + vy2:
        copy.wait_recv()
    for copy in local_copies:
        copy.wait()
    for copy in (
        meta_copies
        + k_copies
        + v_copies
        + sl_copies
        + sy_copies
        + su_copies
        + sv_copies
        + mx_copies
        + my_copies
        + kz1
        + ky1
        + kz2
        + ky2
        + vz1
        + vy1
        + vz2
        + vy2
        + rs_copies
        + yy_copies
        + ag_copies
    ):
        copy.wait_send()


def place_kernel(
    slot_count,
    arrival_ref,
    rows_ref,
    norm_ref,
    k_ref,
    v_ref,
    attended_ref,
    log_norm_ref,
    out_k_ref,
    out_v_ref,
):
    for s in range(STEPS):
        attended_ref[s] = rows_ref[pl.ds(s * REQUESTS, REQUESTS), :]
        log_norm_ref[s] = norm_ref[pl.ds(s * REQUESTS, REQUESTS), pl.ds(0, LOCAL_HEADS * GROUP)]

    def place(s, carry):
        index = arrival_ref[0, s]
        at = jnp.maximum(index - 1, 0)
        there = index > 0
        for ref, out in ((k_ref, out_k_ref), (v_ref, out_v_ref)):
            tile = ref[at].astype(F32)
            wide = jnp.concatenate([tile[:TOK, :], tile[TOK:, :]], axis=1)
            out[s] = jnp.where(there, wide, 0.0).astype(BF16)
        return carry

    lax.fori_loop(0, slot_count, place, 0, unroll=4)


def on_device(
    n_y,
    n_zc,
    prefilled_block_keys,
    prefilled_block_values,
    queries,
    step_token_keys,
    step_token_values,
    lengths,
    block_request,
    block_number,
    owner_rank,
    owner_slot,
    group_first,
):
    n_tp = lax.axis_size("tp")
    own_blocks, _, full_width = prefilled_block_keys.shape
    row_blocks = own_blocks * n_tp
    tokens = own_blocks * TOK
    slot_count = 2 * row_blocks
    n_sp = n_y * n_zc
    chunk = D // n_zc
    smem = pl.BlockSpec(memory_space=pltpu.SMEM)
    vmem = pl.BlockSpec(memory_space=pltpu.VMEM)
    hbm = pl.BlockSpec(memory_space=pltpu.HBM)
    half = n_y // 2
    dma = pltpu.SemaphoreType.DMA
    attended, norms, arrival, kc, vc = pl.pallas_call(
        functools.partial(exchange_kernel, n_y, n_zc, n_tp, own_blocks),
        out_shape=(
            jax.ShapeDtypeStruct((SR, GROUP * PIECE), F32),
            jax.ShapeDtypeStruct((SR, D), F32),
            jax.ShapeDtypeStruct((8, D), jnp.int32),
            jax.ShapeDtypeStruct((2, half, n_zc, 2 * TOK, D), BF16),
            jax.ShapeDtypeStruct((2, half, n_zc, 2 * TOK, D), BF16),
        ),
        in_specs=[smem] * 6 + [vmem] * 3 + [hbm] * 2,
        out_specs=(vmem,) * 5,
        scratch_shapes=[
            pltpu.VMEM((n_tp, 8, D), jnp.int32),
            pltpu.VMEM((n_tp * tokens, PIECE), BF16),
            pltpu.VMEM((n_tp * tokens, PIECE), BF16),
            pltpu.VMEM((row_blocks + 1, TOK, PIECE), F32),
            pltpu.VMEM((row_blocks + 1, TOK, PIECE), F32),
            pltpu.VMEM((8, D), jnp.int32),
            pltpu.SMEM((8, D), jnp.int32),
            pltpu.VMEM((LOCAL_HEADS, n_tp * tokens, ROWS), F32),
            pltpu.VMEM((2, n_zc, half, 2 * TOK, D), BF16),
            pltpu.VMEM((2, n_zc, half, 2 * TOK, D), BF16),
            pltpu.VMEM((2, half, n_zc, 2 * TOK, D), BF16),
            pltpu.VMEM((2, half, n_zc, 2 * TOK, D), BF16),
            pltpu.VMEM((SR, GROUP * PIECE), BF16),
            pltpu.VMEM((SR, PIECE), BF16),
            pltpu.VMEM((SR, PIECE), BF16),
            pltpu.VMEM((n_zc, 1, D), jnp.int32),
            pltpu.VMEM((n_y, n_zc, D), jnp.int32),
            pltpu.VMEM((n_zc, LOCAL_HEADS, ROWS), F32),
            pltpu.VMEM((n_y, LOCAL_HEADS, ROWS), F32),
            pltpu.VMEM((n_zc, LOCAL_HEADS, ROWS), F32),
            pltpu.VMEM((n_y, LOCAL_HEADS, ROWS), F32),
            pltpu.VMEM((n_zc, LOCAL_HEADS * chunk, ROWS), F32),
            pltpu.VMEM((n_zc, LOCAL_HEADS * chunk, ROWS), F32),
            pltpu.VMEM((n_zc, LOCAL_HEADS * chunk, ROWS), F32),
            pltpu.VMEM((n_y, LOCAL_HEADS * chunk, ROWS), F32),
            pltpu.VMEM((n_zc, LOCAL_HEADS * chunk, ROWS), F32),
            dma((7,)),
        ]
        + [dma((n_tp,))] * 6
        + [dma((n_zc,))] * 2
        + [dma((n_y,))] * 2
        + [dma((n_zc,))] * 2
        + [dma((n_y,))] * 2
        + [dma((n_zc,))] * 2
        + [dma((n_y,))] * 2
        + [dma((2, 2, n_zc))] * 2
        + [dma((2, 2, half))] * 2
        + [dma((n_zc,))] * 2
        + [dma((n_y,))] * 2
        + [dma((n_zc,))] * 2,
        compiler_params=pltpu.CompilerParams(
            collective_id=0, has_side_effects=True, vmem_limit_bytes=40 * 2**20
        ),
        name="exchange",
    )(
        block_request,
        block_number,
        owner_rank,
        owner_slot,
        lengths,
        group_first,
        queries,
        step_token_keys,
        step_token_values,
        pltpu.with_memory_space_constraint(prefilled_block_keys.reshape(tokens, full_width), pltpu.HBM),
        pltpu.with_memory_space_constraint(prefilled_block_values.reshape(tokens, full_width), pltpu.HBM),
    )
    slot_shape = jax.ShapeDtypeStruct((slot_count, TOK, PIECE), BF16)
    return pl.pallas_call(
        functools.partial(place_kernel, slot_count),
        out_shape=(
            jax.ShapeDtypeStruct((STEPS, REQUESTS, GROUP * PIECE), F32),
            jax.ShapeDtypeStruct((STEPS, REQUESTS, LOCAL_HEADS * GROUP), F32),
            slot_shape,
            slot_shape,
        ),
        in_specs=[smem] + [vmem] * 4,
        out_specs=(vmem,) * 4,
        compiler_params=pltpu.CompilerParams(vmem_limit_bytes=16 * 2**20),
        name="place",
    )(
        arrival,
        attended,
        norms,
        kc.reshape(n_sp, 2 * TOK, D),
        vc.reshape(n_sp, 2 * TOK, D),
    )


def solution(mesh):
    sp = mesh.shape["sp"]
    n_y = max(2, sp // 16)
    return jax.shard_map(
        functools.partial(on_device, n_y, sp // n_y),
        mesh=mesh,
        in_specs=(
            P(("sp", "tp"), None, None),
            P(("sp", "tp"), None, None),
            P(None, None, "tp"),
            P(None, None, "tp"),
            P(None, None, "tp"),
            P(),
            P(("sp", "tp")),
            P(("sp", "tp")),
            P(("sp", "tp")),
            P(("sp", "tp")),
            P(),
        ),
        out_specs=(
            P(None, None, "tp"),
            P(None, None, "tp"),
            P("sp", None, "tp"),
            P("sp", None, "tp"),
        ),
        check_vma=False,
    )
```

time: 76.2 us -> 63 us (0.83)
  Pallas kernels: 70.2 us -> 59.1 us
  local copies, waits for them, and re-layouts: 5.06 us -> 2.92 us
    pallas_call x1, Pallas kernels: 68.1 us -> 56.9 us  [on_device(): pl.pallas_call(functools.partial(exchange_kernel, n_y, n_zc, n_tp, own_bl...]
    reshape x5 -> x0, local copies, waits for them, and re-layouts: 2.42 us -> none  [the longest x1 0.88 us: on_device(): queries.reshape(SR, GROUP * PIECE)]
    unnamed x19 -> x18, local copies, waits for them, and re-layouts: 2.64 us -> 2.92 us
where the time goes in v2:
time: 63 us; the launch traced here: 62.7 us
  Pallas kernels  59.1 us (94%)
  local copies, waits for them, and re-layouts  2.92 us (5%)
  between operations  0.7 us (1%)
    pallas_call x1, Pallas kernels, on_device(): pl.pallas_call(functools.partial(exchange_kernel, n_y, n_zc, n_tp, own_bl...  56.9 us
    unnamed x18, local copies, waits for them, and re-layouts  2.92 us
    pallas_call x1, Pallas kernels, on_device(): pl.pallas_call(functools.partial(place_kernel, slot_count), out_shape=(ja...  2.2 us

profile of v2, /device:TPU:1, one launch (start us, length us, event | category | flops | bytes accessed | tf_op | source)
XLA Modules:
  0.0 62.7 jit_solution(2444899232458224598)
XLA Ops:
  0.6 0.0 copy-start.6
  0.6 0.0 copy-start.7
  0.7 0.0 copy-start.8
  0.7 0.0 copy-start.3
  0.7 0.0 copy-start.4
  0.7 0.0 copy-start.5
  0.7 0.6 copy-done.6
  1.3 0.0 copy-done.7
  1.3 0.0 copy-done.8
  1.3 0.0 copy-done.3
  1.3 0.0 copy-done.4
  1.4 0.0 copy-done.5
  1.4 0.0 copy-start
  1.4 0.8 %copy-done = bf16[4,4,2048]{2,1,0:T(4,128)(2,1)S(1)} copy-done((bf16[4,4,2048]{2,1,0:T(4,128)(2,1)S(1)}, bf16[4,4,2048]{2,1,0:T(4,128)(2,1)}, u32[]{:S(2)}) %copy-start) | copy-done | bytes 65560
  2.2 0.0 copy-start.1
  2.2 0.7 %copy-done.1 = bf16[4,4,256]{2,1,0:T(4,128)(2,1)S(1)} copy-done((bf16[4,4,256]{2,1,0:T(4,128)(2,1)S(1)}, bf16[4,4,256]{2,1,0:T(4,128)(2,1)}, u32[]{:S(2)}) %copy-start.1) | copy-done | bytes 8216
  2.9 0.0 copy-start.2
  2.9 0.7 %copy-done.2 = bf16[4,4,256]{2,1,0:T(4,128)(2,1)S(1)} copy-done((bf16[4,4,256]{2,1,0:T(4,128)(2,1)S(1)}, bf16[4,4,256]{2,1,0:T(4,128)(2,1)}, u32[]{:S(2)}) %copy-start.2) | copy-done | bytes 8216
  3.6 56.9 %exchange.1 = (f32[16,2048]{1,0:T(8,128)S(1)}, f32[16,128]{1,0:T(8,128)S(1)}, s32[8,128]{1,0:T(8,128)S(1)}, bf16[2,4,16,16,128]{4,3,2,1,0:T(8,128)(2,1)S(1)}, bf16[2,4,16,16,128]{4,3,2,1,0:T(8,128)(2,1)S(1)}) custom-call(s32[16]{0:T(128)S(1)} %copy-done.3, s32[16]{0:T(128)S(1)} %copy-done.4, s32[16]{0:T(128)S(1)} %copy-done.5, s32[16]{0:T(128)S(1)} %copy-done.6, ...), custom_call_target="tpu_custom_call" | custom-call | tf_op jit(solution)/shard_map/exchange/pallas_call | solution.py:565
  60.5 2.2 %place.1 = (f32[4,4,2048]{2,1,0:T(4,128)}, f32[4,4,16]{2,1,0:T(4,128)}, bf16[128,8,256]{2,1,0:T(8,128)(2,1)}, bf16[128,8,256]{2,1,0:T(8,128)(2,1)}) custom-call(s32[8,128]{1,0:T(8,128)S(1)} %get-tuple-element.9.arrival_ref, f32[16,2048]{1,0:T(8,128)S(1)} %get-tuple-element.10.rows_ref, f32[16,128]{1,0:T(8,128)S(1)} %get-tuple-element.11.norm_ref, ...), custom_call_target="tpu_custom_call" | custom-call | tf_op jit(solution)/shard_map/place/pallas_call | solution.py:635
Async XLA Ops:
  0.6 0.7 %copy-start.6 = (s32[16]{0:T(128)S(1)}, s32[16]{0:T(128)}, u32[]{:S(2)}) copy-start(s32[16]{0:T(128)} %slot_ref.1) | copy-start | bytes 196
  0.6 0.7 %copy-start.7 = (s32[4]{0:T(128)S(1)}, s32[4]{0:T(128)}, u32[]{:S(2)}) copy-start(s32[4]{0:T(128)} %lengths_ref.1) | copy-start | bytes 52
  0.7 0.7 %copy-start.8 = (s32[4]{0:T(128)S(1)}, s32[4]{0:T(128)}, u32[]{:S(2)}) copy-start(s32[4]{0:T(128)} %first_ref.1) | copy-start | bytes 52
  0.7 0.7 %copy-start.3 = (s32[16]{0:T(128)S(1)}, s32[16]{0:T(128)}, u32[]{:S(2)}) copy-start(s32[16]{0:T(128)} %request_ref.1) | copy-start | bytes 196
  0.7 0.7 %copy-start.4 = (s32[16]{0:T(128)S(1)}, s32[16]{0:T(128)}, u32[]{:S(2)}) copy-start(s32[16]{0:T(128)} %number_ref.1) | copy-start | bytes 196
  0.7 0.7 %copy-start.5 = (s32[16]{0:T(128)S(1)}, s32[16]{0:T(128)}, u32[]{:S(2)}) copy-start(s32[16]{0:T(128)} %rank_ref.1) | copy-start | bytes 196
  1.4 0.8 %copy-start = (bf16[4,4,2048]{2,1,0:T(4,128)(2,1)S(1)}, bf16[4,4,2048]{2,1,0:T(4,128)(2,1)}, u32[]{:S(2)}) copy-start(bf16[4,4,2048]{2,1,0:T(4,128)(2,1)} %q_ref.1) | copy-start | bytes 196612
  2.2 0.7 %copy-start.1 = (bf16[4,4,256]{2,1,0:T(4,128)(2,1)S(1)}, bf16[4,4,256]{2,1,0:T(4,128)(2,1)}, u32[]{:S(2)}) copy-start(bf16[4,4,256]{2,1,0:T(4,128)(2,1)} %fresh_k_ref.1) | copy-start | bytes 24580
  2.9 0.7 %copy-start.2 = (bf16[4,4,256]{2,1,0:T(4,128)(2,1)S(1)}, bf16[4,4,256]{2,1,0:T(4,128)(2,1)}, u32[]{:S(2)}) copy-start(bf16[4,4,256]{2,1,0:T(4,128)(2,1)} %fresh_v_ref.1) | copy-start | bytes 24580

commit v3 on v2

--- a/solution.py
+++ b/solution.py
@@ -31,15 +31,15 @@
     n_zc,
     n_tp,
     own_blocks,
-    request_ref,
-    number_ref,
-    rank_ref,
-    slot_ref,
-    lengths_ref,
-    first_ref,
-    q_ref,
-    fresh_k_ref,
-    fresh_v_ref,
+    request_hbm,
+    number_hbm,
+    rank_hbm,
+    slot_hbm,
+    lengths_hbm,
+    first_hbm,
+    q_hbm,
+    fresh_k_hbm,
+    fresh_v_hbm,
     keys_ref,
     values_ref,
     attended_ref,
@@ -59,6 +59,16 @@
     kb,
     va,
     vb,
+    request_ref,
+    number_ref,
+    rank_ref,
+    slot_ref,
+    lengths_ref,
+    first_ref,
+    q_ref,
+    fresh_k_ref,
+    fresh_v_ref,
+    operand_sem,
     qs,
     fresh_ks,
     fresh_vs,
@@ -140,12 +150,12 @@
         return copy
 
     barrier = pltpu.get_barrier_semaphore()
-    for k in range(1, n_tp):
-        pl.semaphore_signal(barrier, inc=1, device_id=tp_dev(k), device_id_type=MESH)
-    for k in range(1, n_zc):
-        pl.semaphore_signal(barrier, inc=1, device_id=zc_dev(k), device_id_type=MESH)
-    for j in range(1, n_y):
-        pl.semaphore_signal(barrier, inc=1, device_id=y_dev(j), device_id_type=MESH)
+    distant = [(min(k, n_zc - k) // 2, zc_dev(k)) for k in z_order]
+    distant += [(min(j, n_y - j), y_dev(j)) for j in y_order]
+    distant += [(min(k, n_tp - k), tp_dev(k)) for k in range(1, n_tp)]
+    peers = [dev for _, dev in sorted(distant, key=lambda pair: -pair[0])]
+    for dev in peers:
+        pl.semaphore_signal(barrier, inc=1, device_id=dev, device_id_type=MESH)
 
     def columns(t):
         return pl.ds(pl.multiple_of(t * PIECE, PIECE), PIECE)
@@ -157,6 +167,27 @@
     own_v = pltpu.make_async_copy(values_ref.at[:, columns(tp)], vp.at[rows_of(tp)], local_sem.at[1])
     own_k.start()
     own_v.start()
+
+    fetches = [
+        pltpu.make_async_copy(src, dst, operand_sem.at[n])
+        for n, (src, dst) in enumerate(
+            (
+                (request_hbm, request_ref),
+                (number_hbm, number_ref),
+                (rank_hbm, rank_ref),
+                (slot_hbm, slot_ref),
+                (lengths_hbm, lengths_ref),
+                (first_hbm, first_ref),
+                (q_hbm, q_ref),
+                (fresh_k_hbm, fresh_k_ref),
+                (fresh_v_hbm, fresh_v_ref),
+            )
+        )
+    ]
+    for fetch in fetches:
+        fetch.start()
+    for fetch in fetches:
+        fetch.wait()
 
     lane = lax.broadcasted_iota(jnp.int32, (1, D), 1)
     codes = jnp.full((1, D), REQUESTS, jnp.int32)
@@ -205,7 +236,7 @@
     k32[0] = jnp.zeros((TOK, PIECE), F32)
     v32[0] = jnp.zeros((TOK, PIECE), F32)
 
-    pl.semaphore_wait(barrier, n_tp - 1 + n_zc - 1 + n_y - 1)
+    pl.semaphore_wait(barrier, len(peers))
 
     meta_copies, k_copies, v_copies = [], [], []
     for k in range(1, n_tp):
@@ -262,25 +293,44 @@
 
     half = n_y // 2
     y_starts = [y_at(j) * n_zc for j in range(n_y)]
-    zc_places = [zc_at(k) for k in range(n_zc)]
 
     def source_of(k, j):
-        return src_s[1, y_starts[j] + zc_places[k]]
+        return src_s[1, y_starts[j] + zc_at(k)]
 
     def gather_z(x, staged, k):
         for i in range(half):
             tile = block_tile(staged, source_of(k, 2 * i))
-            if k == 0:
+            if isinstance(k, int):
                 kb[x, 0, i] = tile
             else:
                 ka[x, k, i] = tile
 
     def gather_y(x, staged, i):
-        for k in range(n_zc):
+        def step(k, carry):
             va[x, i, k] = block_tile(staged, source_of(k, 2 * i + 1))
+            return carry
+
+        lax.fori_loop(0, n_zc, step, 0, unroll=4)
+
+    def z_sends(x, staged, first, last):
+        def step(n, carry):
+            away = (n + 1) // 2
+            k = n_zc // 2 + jnp.where(lax.rem(n, 2) == 1, away, -away)
+            gather_z(x, staged, k)
+            z_first(x, k).start()
+            return carry
+
+        lax.fori_loop(first, last, step, 0)
 
     def z_first(x, k):
-        return remote(ka.at[x, k], kb.at[x, k], z_send.at[x, 0, k], z_recv.at[x, 0, k], zc_dev(k))
+        return pltpu.make_async_remote_copy(
+            src_ref=ka.at[x, k],
+            dst_ref=kb.at[x, k],
+            send_sem=z_send.at[x, 0, k],
+            recv_sem=z_recv.at[x, 0, k],
+            device_id=zc_dev(k),
+            device_id_type=MESH,
+        )
 
     def y_first(x, i):
         return remote(
@@ -307,23 +357,21 @@
     k32[pl.ds(1, n_tp * own_blocks)] = kp[...].astype(F32).reshape(n_tp * own_blocks, TOK, PIECE)
     to_scalar.wait()
 
-    kz1, ky1, vz1, vy1 = [], [], [], []
+    ky1, vy1 = [], []
+    kz1 = [z_first(0, k) for k in range(1, n_zc)]
+    vz1 = [z_first(1, k) for k in range(1, n_zc)]
     per = -(-(n_zc - 1) // half)
     for n, i in enumerate(odd_order):
         gather_y(0, k32, i)
         ky1.append(y_first(0, i))
-        for k in z_order[n * per : (n + 1) * per]:
-            gather_z(0, k32, k)
-            kz1.append(z_first(0, k))
+        z_sends(0, k32, n * per, min(n_zc - 1, (n + 1) * per))
     gather_z(0, k32, 0)
 
     own_v.wait()
     for copy in v_copies:
         copy.wait_recv()
     v32[pl.ds(1, n_tp * own_blocks)] = vp[...].astype(F32).reshape(n_tp * own_blocks, TOK, PIECE)
-    for k in z_order:
-        gather_z(1, v32, k)
-        vz1.append(z_first(1, k))
+    z_sends(1, v32, 0, n_zc - 1)
     gather_z(1, v32, 0)
     for i in range(half):
         gather_y(1, v32, i)
@@ -571,7 +619,7 @@
             jax.ShapeDtypeStruct((2, half, n_zc, 2 * TOK, D), BF16),
             jax.ShapeDtypeStruct((2, half, n_zc, 2 * TOK, D), BF16),
         ),
-        in_specs=[smem] * 6 + [vmem] * 3 + [hbm] * 2,
+        in_specs=[hbm] * 11,
         out_specs=(vmem,) * 5,
         scratch_shapes=[
             pltpu.VMEM((n_tp, 8, D), jnp.int32),
@@ -586,6 +634,16 @@
             pltpu.VMEM((2, n_zc, half, 2 * TOK, D), BF16),
             pltpu.VMEM((2, half, n_zc, 2 * TOK, D), BF16),
             pltpu.VMEM((2, half, n_zc, 2 * TOK, D), BF16),
+            pltpu.SMEM((own_blocks,), jnp.int32),
+            pltpu.SMEM((own_blocks,), jnp.int32),
+            pltpu.SMEM((own_blocks,), jnp.int32),
+            pltpu.SMEM((own_blocks,), jnp.int32),
+            pltpu.SMEM((REQUESTS,), jnp.int32),
+            pltpu.SMEM((REQUESTS,), jnp.int32),
+            pltpu.VMEM((STEPS, REQUESTS, GROUP * PIECE), BF16),
+            pltpu.VMEM((STEPS, REQUESTS, PIECE), BF16),
+            pltpu.VMEM((STEPS, REQUESTS, PIECE), BF16),
+            dma((9,)),
             pltpu.VMEM((SR, GROUP * PIECE), BF16),
             pltpu.VMEM((SR, PIECE), BF16),
             pltpu.VMEM((SR, PIECE), BF16),
@@ -619,17 +677,22 @@
         ),
         name="exchange",
     )(
-        block_request,
-        block_number,
-        owner_rank,
-        owner_slot,
-        lengths,
-        group_first,
-        queries,
-        step_token_keys,
-        step_token_values,
-        pltpu.with_memory_space_constraint(prefilled_block_keys.reshape(tokens, full_width), pltpu.HBM),
-        pltpu.with_memory_space_constraint(prefilled_block_values.reshape(tokens, full_width), pltpu.HBM),
+        *[
+            pltpu.with_memory_space_constraint(operand, pltpu.HBM)
+            for operand in (
+                block_request,
+                block_number,
+                owner_rank,
+                owner_slot,
+                lengths,
+                group_first,
+                queries,
+                step_token_keys,
+                step_token_values,
+                prefilled_block_keys.reshape(tokens, full_width),
+                prefilled_block_values.reshape(tokens, full_width),
+            )
+        ]
     )
     slot_shape = jax.ShapeDtypeStruct((slot_count, TOK, PIECE), BF16)
     return pl.pallas_call(

time: 63 us -> 59.5 us (0.944)
  local copies, waits for them, and re-layouts: 2.92 us -> 0 us
    unnamed x18 -> x0, local copies, waits for them, and re-layouts: 2.92 us -> none
where the time goes in v3:
time: 59.5 us; the launch traced here: 59.3 us
  Pallas kernels  58.7 us (99%)
  between operations  0.64 us (1%)
    pallas_call x1, Pallas kernels, on_device(): pl.pallas_call(functools.partial(exchange_kernel, n_y, n_zc, n_tp, own_bl...  56.5 us
    pallas_call x1, Pallas kernels, on_device(): pl.pallas_call(functools.partial(place_kernel, slot_count), out_shape=(ja...  2.2 us

profile of v3, /device:TPU:1, one launch (start us, length us, event | category | flops | bytes accessed | tf_op | source)
XLA Modules:
  0.0 59.3 jit_solution(13975300412135020564)
XLA Ops:
  0.6 56.5 %exchange.1 = (f32[16,2048]{1,0:T(8,128)S(1)}, f32[16,128]{1,0:T(8,128)S(1)}, s32[8,128]{1,0:T(8,128)S(1)}, bf16[2,4,16,16,128]{4,3,2,1,0:T(8,128)(2,1)S(1)}, bf16[2,4,16,16,128]{4,3,2,1,0:T(8,128)(2,1)S(1)}) custom-call(s32[16]{0:T(128)} %request_hbm.1, s32[16]{0:T(128)} %number_hbm.1, s32[16]{0:T(128)} %rank_hbm.1, s32[16]{0:T(128)} %slot_hbm.1, ...), custom_call_target="tpu_custom_call" | custom-call | tf_op jit(solution)/shard_map/exchange/pallas_call | solution.py:613
  57.2 2.2 %place.1 = (f32[4,4,2048]{2,1,0:T(4,128)}, f32[4,4,16]{2,1,0:T(4,128)}, bf16[128,8,256]{2,1,0:T(8,128)(2,1)}, bf16[128,8,256]{2,1,0:T(8,128)(2,1)}) custom-call(s32[8,128]{1,0:T(8,128)S(1)} %get-tuple-element.9.arrival_ref, f32[16,2048]{1,0:T(8,128)S(1)} %get-tuple-element.10.rows_ref, f32[16,128]{1,0:T(8,128)S(1)} %get-tuple-element.11.norm_ref, ...), custom_call_target="tpu_custom_call" | custom-call | tf_op jit(solution)/shard_map/place/pallas_call | solution.py:698

commit v4 on v3

--- a/solution.py
+++ b/solution.py
@@ -394,10 +394,6 @@
     ]
     for i in odd_order:
         vy1.append(y_first(1, i))
-    for copy in kz1:
-        copy.wait_recv()
-    ky2 = [y_second(0, kc, i) for i in even_order]
-    keep(kb.at[0, :, 0], kc.at[0, 0])
     for copy in my_copies:
         copy.wait_recv()
     all_max = my_buf[0]
@@ -427,6 +423,10 @@
     ]
     rs_buf[mzc] = rs_src[mzc]
 
+    for copy in kz1:
+        copy.wait_recv()
+    ky2 = [y_second(0, kc, i) for i in even_order]
+    keep(kb.at[0, :, 0], kc.at[0, 0])
     for copy in ky1:
         copy.wait_recv()
     kz2 = [z_second(0, kc, k) for k in z_order]
@@ -515,42 +515,41 @@
             value = jnp.sum(picked, axis=1, keepdims=True)
             by_head = jnp.where(wide_lane == h * GROUP + g, value, by_head)
     norm_ref[...] = by_head
-    for copy in ag_copies:
-        copy.wait_recv()
-    for h in range(LOCAL_HEADS):
-        by_entry = jnp.concatenate(
-            [ag_buf[p, pl.ds(h * chunk, chunk), :] for p in range(n_zc)], axis=0
-        )
-        by_row = jnp.transpose(by_entry)
-        for g in range(GROUP):
-            attended_ref[:, pl.ds((h * GROUP + g) * D, D)] = by_row[g * SR : (g + 1) * SR, :]
-
-    for copy in kz2 + ky2 + vz2 + vy2:
-        copy.wait_recv()
-    for copy in local_copies:
-        copy.wait()
     for copy in (
         meta_copies
         + k_copies
         + v_copies
         + sl_copies
         + sy_copies
-        + su_copies
-        + sv_copies
         + mx_copies
         + my_copies
         + kz1
         + ky1
-        + kz2
-        + ky2
         + vz1
         + vy1
-        + vz2
-        + vy2
         + rs_copies
+        + su_copies
         + yy_copies
-        + ag_copies
+        + sv_copies
     ):
+        copy.wait_send()
+    for copy in kz2 + ky2:
+        copy.wait()
+    for copy in ag_copies:
+        copy.wait_recv()
+    for h in range(LOCAL_HEADS):
+        by_entry = jnp.concatenate(
+            [ag_buf[p, pl.ds(h * chunk, chunk), :] for p in range(n_zc)], axis=0
+        )
+        by_row = jnp.transpose(by_entry)
+        for g in range(GROUP):
+            attended_ref[:, pl.ds((h * GROUP + g) * D, D)] = by_row[g * SR : (g + 1) * SR, :]
+
+    for copy in vz2 + vy2:
+        copy.wait_recv()
+    for copy in local_copies:
+        copy.wait()
+    for copy in vz2 + vy2 + ag_copies:
         copy.wait_send()
 
 

time: 59.5 us -> 59 us (level)
  Pallas kernels: 58.7 us -> 58.1 us
where the time goes in v4:
time: 59 us; the launch traced here: 58.8 us
  Pallas kernels  58.1 us (98%)
  between operations  0.64 us (1%)
    pallas_call x1, Pallas kernels, on_device(): pl.pallas_call(functools.partial(exchange_kernel, n_y, n_zc, n_tp, own_bl...  55.9 us
    pallas_call x1, Pallas kernels, on_device(): pl.pallas_call(functools.partial(place_kernel, slot_count), out_shape=(ja...  2.2 us

profile of v4, /device:TPU:1, one launch (start us, length us, event | category | flops | bytes accessed | tf_op | source)
XLA Modules:
  0.0 58.8 jit_solution(10609264604505965121)
XLA Ops:
  0.6 55.9 %exchange.1 = (f32[16,2048]{1,0:T(8,128)S(1)}, f32[16,128]{1,0:T(8,128)S(1)}, s32[8,128]{1,0:T(8,128)S(1)}, bf16[2,4,16,16,128]{4,3,2,1,0:T(8,128)(2,1)S(1)}, bf16[2,4,16,16,128]{4,3,2,1,0:T(8,128)(2,1)S(1)}) custom-call(s32[16]{0:T(128)} %request_hbm.1, s32[16]{0:T(128)} %number_hbm.1, s32[16]{0:T(128)} %rank_hbm.1, s32[16]{0:T(128)} %slot_hbm.1, ...), custom_call_target="tpu_custom_call" | custom-call | tf_op jit(solution)/shard_map/exchange/pallas_call | solution.py:612
  56.6 2.2 %place.1 = (f32[4,4,2048]{2,1,0:T(4,128)}, f32[4,4,16]{2,1,0:T(4,128)}, bf16[128,8,256]{2,1,0:T(8,128)(2,1)}, bf16[128,8,256]{2,1,0:T(8,128)(2,1)}) custom-call(s32[8,128]{1,0:T(8,128)S(1)} %get-tuple-element.9.arrival_ref, f32[16,2048]{1,0:T(8,128)S(1)} %get-tuple-element.10.rows_ref, f32[16,128]{1,0:T(8,128)S(1)} %get-tuple-element.11.norm_ref, ...), custom_call_target="tpu_custom_call" | custom-call | tf_op jit(solution)/shard_map/place/pallas_call | solution.py:697

commit v5 on v4

--- a/solution.py
+++ b/solution.py
@@ -385,13 +385,6 @@
     my_copies = [
         remote(my_buf.at[0], my_buf.at[j], my_send.at[j], my_recv.at[j], y_dev(j)) for j in y_order
     ]
-    for copy in sl_copies:
-        copy.wait_recv()
-    for k in range(n_zc):
-        sy[0, pl.ds(k, 1), :] = sl[k]
-    sy_copies = [
-        remote(sy.at[0], sy.at[j], sy_send.at[j], sy_recv.at[j], y_dev(j)) for j in y_order
-    ]
     for i in odd_order:
         vy1.append(y_first(1, i))
     for copy in my_copies:
@@ -427,6 +420,13 @@
         copy.wait_recv()
     ky2 = [y_second(0, kc, i) for i in even_order]
     keep(kb.at[0, :, 0], kc.at[0, 0])
+    for copy in sl_copies:
+        copy.wait_recv()
+    for k in range(n_zc):
+        sy[0, pl.ds(k, 1), :] = sl[k]
+    sy_copies = [
+        remote(sy.at[0], sy.at[j], sy_send.at[j], sy_recv.at[j], y_dev(j)) for j in y_order
+    ]
     for copy in ky1:
         copy.wait_recv()
     kz2 = [z_second(0, kc, k) for k in z_order]
@@ -442,6 +442,55 @@
         for p in range(n_zc):
             fresh_num[p, pl.ds(h * chunk, chunk), :] = number[p * chunk : (p + 1) * chunk, :]
 
+
+    for copy in rs_copies:
+        copy.wait_recv()
+    part = rs_buf[0]
+    for p in range(1, n_zc):
+        part = part + rs_buf[p]
+    yy_buf[my] = part
+    yy_copies = [
+        remote(yy_buf.at[my], yy_buf.at[my], yy_send.at[j], yy_recv.at[j], y_dev(j)) for j in y_order
+    ]
+    for copy in su_copies:
+        copy.wait_recv()
+    part = su[0]
+    for p in range(1, n_zc):
+        part = part + su[p]
+    sv[my] = part
+    sv_copies = [
+        remote(sv.at[my], sv.at[my], sv_send.at[j], sv_recv.at[j], y_dev(j)) for j in y_order
+    ]
+
+    for copy in vz1:
+        copy.wait_recv()
+    vy2 = [y_second(1, vc, i) for i in even_order]
+    keep(kb.at[1, :, 0], vc.at[0, 0])
+    for copy in vy1:
+        copy.wait_recv()
+    vz2 = [z_second(1, vc, k) for k in z_order[: n_zc // 2]]
+    keep(vb.at[1, :, 0], vc.at[1, :, 0])
+
+    for copy in yy_copies:
+        copy.wait_recv()
+    whole = yy_buf[0]
+    for copy in sv_copies:
+        copy.wait_recv()
+    sums = sv[0]
+    for j in range(1, n_y):
+        whole = whole + yy_buf[j]
+        sums = sums + sv[j]
+    norms = []
+    for h in range(LOCAL_HEADS):
+        total = sums[h : h + 1, :] + fresh_totals[h]
+        number = whole[h * chunk : (h + 1) * chunk, :] + fresh_num[mzc, pl.ds(h * chunk, chunk), :]
+        ag_buf[mzc, pl.ds(h * chunk, chunk), :] = number / total
+        norms.append(row_tops[h] + jnp.log(total))
+    ag_copies = [
+        remote(ag_buf.at[mzc], ag_buf.at[mzc], ag_send.at[k], ag_recv.at[k], zc_dev(k))
+        for k in z_order
+    ]
+    vz2 += [z_second(1, vc, k) for k in z_order[n_zc // 2 :]]
     for copy in sy_copies:
         copy.wait_recv()
     column = []
@@ -457,55 +506,6 @@
     for j in range(1, n_y):
         arrival = jnp.maximum(arrival, column[j])
     arrival_ref[...] = jnp.broadcast_to(arrival, (8, D))
-
-    for copy in rs_copies:
-        copy.wait_recv()
-    part = rs_buf[0]
-    for p in range(1, n_zc):
-        part = part + rs_buf[p]
-    yy_buf[my] = part
-    yy_copies = [
-        remote(yy_buf.at[my], yy_buf.at[my], yy_send.at[j], yy_recv.at[j], y_dev(j)) for j in y_order
-    ]
-    for copy in su_copies:
-        copy.wait_recv()
-    part = su[0]
-    for p in range(1, n_zc):
-        part = part + su[p]
-    sv[my] = part
-    sv_copies = [
-        remote(sv.at[my], sv.at[my], sv_send.at[j], sv_recv.at[j], y_dev(j)) for j in y_order
-    ]
-
-    for copy in vz1:
-        copy.wait_recv()
-    vy2 = [y_second(1, vc, i) for i in even_order]
-    keep(kb.at[1, :, 0], vc.at[0, 0])
-    for copy in vy1:
-        copy.wait_recv()
-    vz2 = [z_second(1, vc, k) for k in z_order[: n_zc // 2]]
-    keep(vb.at[1, :, 0], vc.at[1, :, 0])
-
-    for copy in yy_copies:
-        copy.wait_recv()
-    whole = yy_buf[0]
-    for copy in sv_copies:
-        copy.wait_recv()
-    sums = sv[0]
-    for j in range(1, n_y):
-        whole = whole + yy_buf[j]
-        sums = sums + sv[j]
-    norms = []
-    for h in range(LOCAL_HEADS):
-        total = sums[h : h + 1, :] + fresh_totals[h]
-        number = whole[h * chunk : (h + 1) * chunk, :] + fresh_num[mzc, pl.ds(h * chunk, chunk), :]
-        ag_buf[mzc, pl.ds(h * chunk, chunk), :] = number / total
-        norms.append(row_tops[h] + jnp.log(total))
-    ag_copies = [
-        remote(ag_buf.at[mzc], ag_buf.at[mzc], ag_send.at[k], ag_recv.at[k], zc_dev(k))
-        for k in z_order
-    ]
-    vz2 += [z_second(1, vc, k) for k in z_order[n_zc // 2 :]]
     wide_lane = lax.broadcasted_iota(jnp.int32, (SR, D), 1)
     wide_row = lax.broadcasted_iota(jnp.int32, (SR, D), 0)
     by_head = jnp.zeros((SR, D), F32)
@@ -579,7 +579,7 @@
             out[s] = jnp.where(there, wide, 0.0).astype(BF16)
         return carry
 
-    lax.fori_loop(0, slot_count, place, 0, unroll=4)
+    lax.fori_loop(0, slot_count, place, 0, unroll=16)
 
 
 def on_device(

time: 59 us -> 58.6 us (level)
  no operation moved by 1% of the time
where the time goes in v5:
time: 58.6 us; the launch traced here: 58.5 us
  Pallas kernels  57.8 us (99%)
  between operations  0.64 us (1%)
    pallas_call x1, Pallas kernels, on_device(): pl.pallas_call(functools.partial(exchange_kernel, n_y, n_zc, n_tp, own_bl...  55.8 us
    pallas_call x1, Pallas kernels, on_device(): pl.pallas_call(functools.partial(place_kernel, slot_count), out_shape=(ja...  2.05 us

profile of v5, /device:TPU:1, one launch (start us, length us, event | category | flops | bytes accessed | tf_op | source)
XLA Modules:
  0.0 58.5 jit_solution(659478600776009650)
XLA Ops:
  0.6 55.8 %exchange.1 = (f32[16,2048]{1,0:T(8,128)S(1)}, f32[16,128]{1,0:T(8,128)S(1)}, s32[8,128]{1,0:T(8,128)S(1)}, bf16[2,4,16,16,128]{4,3,2,1,0:T(8,128)(2,1)S(1)}, bf16[2,4,16,16,128]{4,3,2,1,0:T(8,128)(2,1)S(1)}) custom-call(s32[16]{0:T(128)} %request_hbm.1, s32[16]{0:T(128)} %number_hbm.1, s32[16]{0:T(128)} %rank_hbm.1, s32[16]{0:T(128)} %slot_hbm.1, ...), custom_call_target="tpu_custom_call" | custom-call | tf_op jit(solution)/shard_map/exchange/pallas_call | solution.py:612
  56.4 2.0 %place.1 = (f32[4,4,2048]{2,1,0:T(4,128)}, f32[4,4,16]{2,1,0:T(4,128)}, bf16[128,8,256]{2,1,0:T(8,128)(2,1)}, bf16[128,8,256]{2,1,0:T(8,128)(2,1)}) custom-call(s32[8,128]{1,0:T(8,128)S(1)} %get-tuple-element.9.arrival_ref, f32[16,2048]{1,0:T(8,128)S(1)} %get-tuple-element.10.rows_ref, f32[16,128]{1,0:T(8,128)S(1)} %get-tuple-element.11.norm_ref, ...), custom_call_target="tpu_custom_call" | custom-call | tf_op jit(solution)/shard_map/place/pallas_call | solution.py:697

commit v6 on v5

--- a/solution.py
+++ b/solution.py
@@ -238,16 +238,17 @@
 
     pl.semaphore_wait(barrier, len(peers))
 
+    x_order = sorted(range(1, n_tp), key=lambda k: -min(k, n_tp - k))
     meta_copies, k_copies, v_copies = [], [], []
-    for k in range(1, n_tp):
+    for k in x_order:
         meta_copies.append(
             remote(meta.at[tp], meta.at[tp], meta_send.at[k], meta_recv.at[k], tp_dev(k))
         )
-    for k in range(1, n_tp):
+    for k in x_order:
         k_copies.append(
             remote(keys_ref.at[:, columns(tp_at(k))], kp.at[rows_of(tp)], kp_send.at[k], kp_recv.at[k], tp_dev(k))
         )
-    for k in range(1, n_tp):
+    for k in x_order:
         v_copies.append(
             remote(
                 values_ref.at[:, columns(tp_at(k))], vp.at[rows_of(tp)], vp_send.at[k], vp_recv.at[k], tp_dev(k)

time: 58.6 us -> 59.9 us (1.022)
  Pallas kernels: 57.8 us -> 59.1 us
    pallas_call x1, Pallas kernels: 55.8 us -> 57.1 us  [on_device(): pl.pallas_call(functools.partial(exchange_kernel, n_y, n_zc, n_tp, own_bl...]
where the time goes in v6:
time: 59.9 us; the launch traced here: 59.8 us
  Pallas kernels  59.1 us (99%)
  between operations  0.64 us (1%)
    pallas_call x1, Pallas kernels, on_device(): pl.pallas_call(functools.partial(exchange_kernel, n_y, n_zc, n_tp, own_bl...  57.1 us
    pallas_call x1, Pallas kernels, on_device(): pl.pallas_call(functools.partial(place_kernel, slot_count), out_shape=(ja...  2.05 us

profile of v6, /device:TPU:1, one launch (start us, length us, event | category | flops | bytes accessed | tf_op | source)
XLA Modules:
  0.0 59.8 jit_solution(13604296366127640440)
XLA Ops:
  0.6 57.1 %exchange.1 = (f32[16,2048]{1,0:T(8,128)S(1)}, f32[16,128]{1,0:T(8,128)S(1)}, s32[8,128]{1,0:T(8,128)S(1)}, bf16[2,4,16,16,128]{4,3,2,1,0:T(8,128)(2,1)S(1)}, bf16[2,4,16,16,128]{4,3,2,1,0:T(8,128)(2,1)S(1)}) custom-call(s32[16]{0:T(128)} %request_hbm.1, s32[16]{0:T(128)} %number_hbm.1, s32[16]{0:T(128)} %rank_hbm.1, s32[16]{0:T(128)} %slot_hbm.1, ...), custom_call_target="tpu_custom_call" | custom-call | tf_op jit(solution)/shard_map/exchange/pallas_call | solution.py:613
  57.7 2.0 %place.1 = (f32[4,4,2048]{2,1,0:T(4,128)}, f32[4,4,16]{2,1,0:T(4,128)}, bf16[128,8,256]{2,1,0:T(8,128)(2,1)}, bf16[128,8,256]{2,1,0:T(8,128)(2,1)}) custom-call(s32[8,128]{1,0:T(8,128)S(1)} %get-tuple-element.9.arrival_ref, f32[16,2048]{1,0:T(8,128)S(1)} %get-tuple-element.10.rows_ref, f32[16,128]{1,0:T(8,128)S(1)} %get-tuple-element.11.norm_ref, ...), custom_call_target="tpu_custom_call" | custom-call | tf_op jit(solution)/shard_map/place/pallas_call | solution.py:698
